TPU v7x, 256 devices: a whole 4x4x8 slice. The times are simulated.
256 devices in a mesh: dp: 8 (over z_hi, y), px: 4 (over x), py: 8 (over z_lo, core).
Axes of the slice: x: 4, y: 4, z: 8 (z_hi: 2, z_lo: 4; z = z_hi * 4 + z_lo), core: 2. Of those that a mesh axis runs over, the one named last changes fastest.
Arguments:
- fields: bfloat16 [8, 24, 128, 128, 128], P('dp', None, 'px', 'py'), may hold values from -6 to 6
- cotangent: bfloat16 [8, 24, 128, 128, 128], P('dp', None, 'px', 'py'), may hold values from -6 to 6
- spectral_weight: bfloat16 [1024, 16, 2, 576], P(('px', 'py')), may hold values from -6 to 6
- bypass: bfloat16 [24, 24], replicated, may hold values from -1.25 to 1.25
Outputs:
- grad_weight: float32 [1024, 16, 2, 576], P(('px', 'py'))
- grad_fields: bfloat16 [8, 24, 128, 128, 128], P('dp', None, 'px', 'py')
All inputs are finite; a program needn't handle non-finite values.
Results may differ from a plain program's by a relative error of at most 0.025.
Values may be sent and summed in bfloat16 or wider, within the bound.
A program may use at most 192 MiB of HBM per device.

v0:
```python
import math

import jax
import jax.numpy as jnp
import numpy as np
from jax import lax
from jax.sharding import PartitionSpec as P

MODES = 16
NX = 128
NY = 128
NZ = 128


def axis_table(length, mode_count):
    grid_pos = np.arange(length)
    kept_freq = np.concatenate([np.arange(mode_count), np.arange(length - mode_count, length)])
    angles = 2.0 * math.pi * (kept_freq[None, :] * grid_pos[:, None] % length) / length
    norm_scale = length ** (-0.5)
    cosine = np.cos(angles) * norm_scale
    sine_part = np.sin(angles) * norm_scale
    result = np.zeros((2, length, 2, 2 * mode_count))
    result[0, :, 0, :] = cosine
    result[1, :, 0, :] = sine_part
    result[0, :, 1, :] = -sine_part
    result[1, :, 1, :] = cosine
    return jnp.asarray(result, jnp.float32).astype(jnp.bfloat16)


def depth_tables(length, mode_count):
    grid_pos = np.arange(length)
    frequency = np.arange(mode_count)
    angles = 2.0 * math.pi * (frequency[None, :] * grid_pos[:, None] % length) / length
    norm_scale = length ** (-0.5)
    result = np.zeros((length, mode_count, 2))
    result[:, :, 0] = np.cos(angles) * norm_scale
    result[:, :, 1] = -np.sin(angles) * norm_scale
    result = result.reshape(length, 2 * mode_count)
    doubling = np.repeat(np.where(frequency == 0, 1.0, 2.0), 2)
    plain = jnp.asarray(result, jnp.float32).astype(jnp.bfloat16)
    doubled = jnp.asarray(result * doubling[None, :], jnp.float32).astype(jnp.bfloat16)
    return (plain, doubled)


def gelu_slope(values):
    normal_cdf = 0.5 * (1.0 + lax.erf(values * 0.7071067811865476))
    density = jnp.exp(-0.5 * values * values) * 0.3989422804014327
    return normal_cdf + values * density


def mixing(form, left, right):
    return jnp.einsum(form, left, right, preferred_element_type=jnp.float32)


def shards(fields, cotangent, spectral_weight, bypass):
    count_x = lax.axis_size("px")
    count_y = lax.axis_size("py")
    devices_plane = count_x * count_y
    samples, channels, x_local, y_local, depth_len = fields.shape
    modes_local = spectral_weight.shape[0]
    group_size = samples * channels * 2 * MODES // devices_plane
    block_cells = x_local * y_local
    depth_cut, depth_double = depth_tables(NZ, MODES)
    cross_cut = axis_table(NX, MODES).reshape(2, count_x, x_local, 2, 2 * MODES)
    along_cut = axis_table(NY, MODES).reshape(2, count_y, y_local, 2, 2 * MODES)

    def to_slab(blocks):
        merged = blocks.reshape(devices_plane, group_size, block_cells)
        moved = lax.all_to_all(merged, ("px", "py"), split_axis=0, concat_axis=0, tiled=True)
        return moved.reshape(count_x, count_y, group_size, block_cells)

    def to_pencil(blocks):
        merged = blocks.reshape(devices_plane, group_size, block_cells)
        moved = lax.all_to_all(merged, ("px", "py"), split_axis=0, concat_axis=0, tiled=True)
        return moved.reshape(count_x, count_y, group_size, block_cells)

    def to_modes(source, table):
        lines = mixing("bcxyn,nq->bcqxy", source, table).astype(jnp.bfloat16)
        blocks = lines.reshape(count_x, count_y, group_size, block_cells)
        slab_data = to_slab(blocks).reshape(count_x, count_y, group_size // 2, 2, x_local, y_local)
        row_modes = mixing("pqgrxy,rqysk->pgsxk", slab_data, along_cut).astype(jnp.bfloat16)
        plane_modes = mixing("pgsxk,spxtj->gtjk", row_modes, cross_cut).astype(jnp.bfloat16)
        spread = plane_modes.reshape(group_size, devices_plane, modes_local)
        gathered = lax.all_to_all(spread, ("px", "py"), split_axis=1, concat_axis=0, tiled=True)
        return gathered.reshape(samples, channels, MODES, 2, modes_local)

    def from_modes(spectrum, table):
        spread = spectrum.reshape(devices_plane, group_size, 1, modes_local)
        returned = lax.all_to_all(spread, ("px", "py"), split_axis=0, concat_axis=2, tiled=True)
        plane_modes = returned.reshape(group_size // 2, 2, 2 * MODES, 2 * MODES)
        row_modes = mixing("gtjk,rpxtj->pgrxk", plane_modes, cross_cut).astype(jnp.bfloat16)
        slab_data = mixing("pgsxk,rqysk->pqgrxy", row_modes, along_cut).astype(jnp.bfloat16)
        blocks = slab_data.reshape(count_x, count_y, group_size, block_cells)
        pencil = to_pencil(blocks).reshape(samples, channels, 2 * MODES, x_local, y_local)
        return mixing("bcqxy,nq->bcxyn", pencil, table)

    weights = spectral_weight.reshape(modes_local, MODES, 2, channels, channels)
    weight_re = weights[:, :, 0]
    weight_im = weights[:, :, 1]
    field_hat = to_modes(fields, depth_cut)
    field_re = field_hat[:, :, :, 0]
    field_im = field_hat[:, :, :, 1]
    mixed_re = mixing("mzio,bizm->bozm", weight_re, field_re) - mixing(
        "mzio,bizm->bozm", weight_im, field_im
    )
    mixed_im = mixing("mzio,bizm->bozm", weight_re, field_im) + mixing(
        "mzio,bizm->bozm", weight_im, field_re
    )
    mixed_hat = jnp.stack([mixed_re, mixed_im], axis=3).astype(jnp.bfloat16)
    pre_act = from_modes(mixed_hat, depth_double) + mixing("oc,bcxyn->boxyn", bypass, fields)
    gprime = (cotangent.astype(jnp.float32) * gelu_slope(pre_act)).astype(jnp.bfloat16)
    grad_hat = to_modes(gprime, depth_double)
    grad_re = grad_hat[:, :, :, 0]
    grad_im = grad_hat[:, :, :, 1]
    part_real = mixing("bozm,bizm->mzio", grad_re, field_re) + mixing(
        "bozm,bizm->mzio", grad_im, field_im
    )
    part_imag = mixing("bozm,bizm->mzio", grad_im, field_re) - mixing(
        "bozm,bizm->mzio", grad_re, field_im
    )
    local_terms = jnp.stack([part_real, part_imag], axis=2).reshape(
        modes_local, MODES, 2, channels * channels
    )
    grad_weight = lax.psum(local_terms.astype(jnp.bfloat16), "dp").astype(jnp.float32)
    back_re = mixing("mzio,bozm->bizm", weight_re, grad_re) + mixing(
        "mzio,bozm->bizm", weight_im, grad_im
    )
    back_im = mixing("mzio,bozm->bizm", weight_re, grad_im) - mixing(
        "mzio,bozm->bizm", weight_im, grad_re
    )
    back_hat = jnp.stack([back_re, back_im], axis=3).astype(jnp.bfloat16)
    grad_fields = from_modes(back_hat, depth_cut) + mixing("oc,boxyn->bcxyn", bypass, gprime)
    return (grad_weight, grad_fields.astype(jnp.bfloat16))


def solution(mesh):
    in_specs = (
        P("dp", None, "px", "py", None),
        P("dp", None, "px", "py", None),
        P(("px", "py"), None, None, None),
        P(),
    )
    out_specs = (P(("px", "py"), None, None, None), P("dp", None, "px", "py", None))
    return jax.shard_map(shards, mesh=mesh, in_specs=in_specs, out_specs=out_specs, check_vma=False)
```

profile of v0, /device:TPU:2, one launch (start us, length us, event | category | flops | bytes accessed | tf_op | source)
XLA Modules:
  0.0 459.3 jit_solution(10196593437112407022)
XLA Ops:
  7.2 7.0 %convert_bitcast_fusion.1 = bf16[1,24,32,32,16]{3,2,4,1,0:T(8,128)(2,1)S(1)} fusion(bf16[128,32,1,1]{0,1,3,2:T(8,128)(2,1)} %constant.34, bf16[24,32,16,128]{3,2,1,0:T(8,128)(2,1)} %bitcast.332), kind=kOutput, calls=%fused_computation.47 | convolution fusion | flops 101056512 | bytes 3940352 | tf_op jit(solution)/shard_map/bcxyn,nq->bcqxy/dot_general | solution.py:52
  19.7 11.1 %reshape_reshape.20 = bf16[32,24,512]{2,1,0:T(8,128)(2,1)S(1)} reshape(bf16[1,24,32,32,16]{4,3,2,1,0:T(8,128)(2,1)} %copy.71) | data formatting | bytes 1572864 | tf_op jit(solution)/shard_map/reshape;reshape | solution.py:68
  30.8 28.7 %all_to_all.80 = bf16[32,24,512]{2,1,0:T(8,128)(2,1)S(1)} all-to-all(bf16[32,24,512]{2,1,0:T(8,128)(2,1)S(1)} %reshape_reshape.20), channel_id=1, replica_groups=mesh['dp'=8,'px'=4,'py'=8] {'px','py'}, dimensions={0} | all-to-all | bytes 1572864 | tf_op jit(solution)/shard_map/all_to_all | solution.py:69
  59.4 6.4 %reshape_reshape.21 = bf16[4,8,12,2,32,16]{5,4,3,2,1,0:T(8,128)(2,1)} reshape(bf16[32,24,512]{2,1,0:T(8,128)(2,1)S(1)} %all_to_all.80) | data formatting | bytes 1572864 | tf_op jit(solution)/shard_map/reshape;reshape | solution.py:80
  71.2 6.6 %all-to-all-start.1 = ((bf16[32,2,384]{2,1,0:T(2,128)(2,1)}), bf16[32,2,384]{2,1,0:T(2,128)(2,1)S(1)}, u32[]{:S(2)}, u32[]{:S(2)}) async-start(bf16[32,2,384]{2,1,0:T(2,128)(2,1)} %reshape.227), calls=%async_computation.1 | async-start | bytes 98304 | tf_op jit(solution)/shard_map/all_to_all | solution.py:84
  77.9 6.4 %reshape.174 = bf16[32,16,2,24,24]{4,3,1,2,0:T(8,128)(2,1)} reshape(bf16[32,16,2,576]{3,1,2,0:T(8,128)(2,1)S(1)} %copy.76) | data formatting | bytes 2359296 | tf_op jit(solution)/shard_map/reshape | solution.py:97
  86.1 9.3 %fusion.2 = (f32[16,32,24]{2,0,1:T(8,128)S(1)}, f32[16,32,24]{2,0,1:T(8,128)S(1)}, f32[16,32,24]{2,0,1:T(8,128)S(1)}, f32[16,32,24]{2,0,1:T(8,128)S(1)}) fusion(f32[16,32,24]{2,0,1:T(8,128)S(1)} %copy.220, bf16[32,16,2,24,24]{4,3,1,2,0:T(8,128)(2,1)} %reshape.174, f32[16,32,24]{2,0,1:T(8,128)S(1)} %copy.219), kind=kLoop, calls=%fused_computation.11 | loop fusion | flops 2899968 | bytes 1474560
  96.6 14.3 %all_to_all.81 = bf16[32,2,384]{2,1,0:T(2,128)(2,1)S(1)} all-to-all(bf16[32,2,384]{2,1,0:T(2,128)(2,1)S(1)} %reshape.229), channel_id=1, replica_groups=mesh['dp'=8,'px'=4,'py'=8] {'px','py'}, dimensions={0} | all-to-all | bytes 98304 | tf_op jit(solution)/shard_map/all_to_all | solution.py:89
  118.2 11.9 %reshape_reshape.22 = bf16[32,24,512]{2,1,0:T(8,128)(2,1)} reshape(bf16[4,8,12,2,32,16]{5,4,3,2,1,0:T(8,128)(2,1)} %copy.83) | data formatting | bytes 1572864 | tf_op jit(solution)/shard_map/reshape;reshape | solution.py:73
  140.8 15.1 %all-to-all-done.3 = bf16[32,24,512]{2,1,0:T(8,128)(2,1)} async-done(((bf16[32,24,512]{2,1,0:T(8,128)(2,1)}), bf16[32,24,512]{2,1,0:T(8,128)(2,1)}, u32[]{:S(2)}, u32[]{:S(2)}) %all-to-all-start.3) | async-done | bytes 786464 | tf_op jit(solution)/shard_map/all_to_all | solution.py:74
  155.8 7.6 %reshape.177 = bf16[24,32,32,16]{3,2,1,0:T(8,128)(2,1)} reshape(bf16[32,24,512]{2,1,0:T(8,128)(2,1)} %all-to-all-done.3) | data formatting | bytes 1572864 | tf_op jit(solution)/shard_map/reshape.24
  163.4 8.4 %fusion.31 = bf16[24,32,16,128]{3,2,1,0:T(8,128)(2,1)S(1)} fusion(f32[32,16,128,24]{2,3,1,0:T(8,128)} %fusion.27, bf16[1,24,32,16,128]{4,3,2,1,0:T(8,128)(2,1)S(1)} %copy-done.8, bf16[128,32,1,1]{0,1,3,2:T(8,128)(2,1)S(1)} %copy-done.7, bf16[24,32,32,16]{3,2,1,0:T(8,128)(2,1)} %reshape.177), kind=kOutput, calls=%fused_computation.48 | convolution fusion | flops 119537664 | bytes 13377536 | tf_op jit(solution)/shard_map/bcqxy,nq->bcxyn/dot_general | solution.py:52
  174.5 9.8 %copy.87 = bf16[1,24,32,32,16]{4,3,2,1,0:T(8,128)(2,1)} copy(bf16[1,24,32,32,16]{2,4,3,1,0:T(8,128)(2,1)S(1)} %convert_bitcast_fusion) | data formatting | bytes 1572864 | tf_op jit(solution)/shard_map/convert_element_type | solution.py:78
  184.3 11.1 %reshape_reshape.23 = bf16[32,24,512]{2,1,0:T(8,128)(2,1)S(1)} reshape(bf16[1,24,32,32,16]{4,3,2,1,0:T(8,128)(2,1)} %copy.87) | data formatting | bytes 1572864 | tf_op jit(solution)/shard_map/reshape;reshape | solution.py:68
  195.4 26.4 %all_to_all.82 = bf16[32,24,512]{2,1,0:T(8,128)(2,1)S(1)} all-to-all(bf16[32,24,512]{2,1,0:T(8,128)(2,1)S(1)} %reshape_reshape.23), channel_id=1, replica_groups=mesh['dp'=8,'px'=4,'py'=8] {'px','py'}, dimensions={0} | all-to-all | bytes 1572864 | tf_op jit(solution)/shard_map/all_to_all | solution.py:69
  221.8 6.4 %reshape_reshape.24 = bf16[4,8,12,2,32,16]{5,4,3,2,1,0:T(8,128)(2,1)} reshape(bf16[32,24,512]{2,1,0:T(8,128)(2,1)S(1)} %all_to_all.82) | data formatting | bytes 1572864 | tf_op jit(solution)/shard_map/reshape;reshape | solution.py:80
  232.8 12.8 %all_to_all.83 = bf16[32,2,384]{2,1,0:T(2,128)(2,1)S(1)} all-to-all(bf16[32,2,384]{2,1,0:T(2,128)(2,1)S(1)} %reshape.231), channel_id=1, replica_groups=mesh['dp'=8,'px'=4,'py'=8] {'px','py'}, dimensions={0} | all-to-all | bytes 98304 | tf_op jit(solution)/shard_map/all_to_all | solution.py:84
  246.6 8.6 %fusion.6 = (f32[16,32,24]{2,0,1:T(8,128)S(1)}, f32[16,32,24]{2,0,1:T(8,128)S(1)}, f32[16,32,24]{2,0,1:T(8,128)S(1)}, f32[16,32,24]{2,0,1:T(8,128)S(1)}) fusion(f32[16,32,24]{2,0,1:T(8,128)S(1)} %copy.222, bf16[32,16,2,24,24]{4,3,1,2,0:T(8,128)(2,1)} %reshape.174, f32[16,32,24]{2,0,1:T(8,128)S(1)} %copy.221), kind=kLoop, calls=%fused_computation.15 | loop fusion | flops 2899968 | bytes 1474560
  277.0 11.7 %reshape_reshape.25 = bf16[32,24,512]{2,1,0:T(8,128)(2,1)} reshape(bf16[4,8,12,2,32,16]{5,4,3,2,1,0:T(8,128)(2,1)} %copy.100) | data formatting | bytes 1572864 | tf_op jit(solution)/shard_map/reshape;reshape | solution.py:73
  294.6 6.9 %add_convert_fusion = (bf16[32,16,24,24]{3,2,1,0:T(8,128)(2,1)}, bf16[32,16,24,24]{3,2,1,0:T(8,128)(2,1)S(1)}) fusion(f32[32,16,24]{2,1,0:T(8,128)} %copy.93, f32[32,16,24]{2,1,0:T(8,128)} %copy.92, f32[32,16,24]{2,1,0:T(8,128)} %copy.91, f32[32,16,24]{2,1,0:T(8,128)S(1)} %copy.75), kind=kLoop, calls=%fused_computation.37 | loop fusion | flops 2359296 | bytes 1376256 | tf_op jit(solution)/shard_map/convert.27
  311.7 6.5 %fusion.25 = f32[32,16,128,24]{2,3,1,0:T(8,128)} fusion(bf16[24,32,16,128]{3,2,1,0:T(8,128)(2,1)} %copy-done.2, bf16[24,24]{1,0:T(8,128)(2,1)S(1)} %copy-done), kind=kOutput, calls=%fused_computation.40 | convolution fusion | flops 75497472 | bytes 9438336 | tf_op jit(solution)/shard_map/oc,boxyn->bcxyn/dot_general | solution.py:52
  318.3 113.4 %all-reduce.2.cloned.1.call-done = bf16[32,16,2,576]{3,1,0,2:T(8,128)(2,1)} async-done(((bf16[32,16,2,576]{3,1,0,2:T(8,128)(2,1)}), bf16[32,16,2,576]{3,1,0,2:T(8,128)(2,1)}) %all-reduce.2.cloned.1.call-update) | async-done | bytes 1179664 | tf_op jit(solution)/shard_map/psum | solution.py:124
  435.8 7.6 %reshape.184 = bf16[24,32,32,16]{3,2,1,0:T(8,128)(2,1)} reshape(bf16[32,24,512]{2,1,0:T(8,128)(2,1)} %all-to-all-done.7) | data formatting | bytes 1572864 | tf_op jit(solution)/shard_map/reshape.50
  443.4 8.9 %fusion.14 = bf16[1,24,32,16,128]{4,3,2,1,0:T(8,128)(2,1)} fusion(f32[32,16,128,24]{2,3,1,0:T(8,128)} %fusion.25, bf16[128,32,1,1]{0,1,3,2:T(8,128)(2,1)S(1)} %copy-done.6, bf16[24,32,32,16]{3,2,1,0:T(8,128)(2,1)} %reshape.184), kind=kOutput, calls=%fused_computation.24 | convolution fusion | flops 103809024 | bytes 10231808 | tf_op jit(solution)/shard_map/bcqxy,nq->bcxyn/dot_general | solution.py:52
  (93 shorter events, 81.7 us)
Async XLA Ops:
  7.2 129.0 %copy-start = (bf16[24,24]{1,0:T(8,128)(2,1)S(1)}, bf16[24,24]{1,0:T(8,128)(2,1)}, u32[]{:S(2)}) copy-start(bf16[24,24]{1,0:T(8,128)(2,1)} %param.11) | copy-start | bytes 3460
  19.7 46.1 %copy-start.10 = (bf16[2,8,16,2,32,1,1]{4,2,0,1,3,5,6:T(8,128)(2,1)S(1)}, bf16[2,8,16,2,32,1,1]{4,2,0,1,3,5,6:T(8,128)(2,1)}, u32[]{:S(2)}) copy-start(bf16[2,8,16,2,32,1,1]{4,2,0,1,3,5,6:T(8,128)(2,1)} %constant.35) | copy-start | bytes 98308
  19.7 46.2 %copy-start.12 = (bf16[2,4,32,2,32,1]{4,2,0,1,3,5:T(8,128)(2,1)S(1)}, bf16[2,4,32,2,32,1]{4,2,0,1,3,5:T(8,128)(2,1)}, u32[]{:S(2)}) copy-start(bf16[2,4,32,2,32,1]{4,2,0,1,3,5:T(8,128)(2,1)} %constant.36) | copy-start | bytes 98308
  65.8 12.0 %copy-start.3 = (bf16[32,16,2,576]{3,2,1,0:T(2,128)(2,1)S(1)}, bf16[32,16,2,576]{3,2,1,0:T(2,128)(2,1)}, u32[]{:S(2)}) copy-start(bf16[32,16,2,576]{3,2,1,0:T(2,128)(2,1)} %param.10) | copy-start | bytes 3538948
  71.2 13.3 %all-to-all-start.1 = ((bf16[32,2,384]{2,1,0:T(2,128)(2,1)}), bf16[32,2,384]{2,1,0:T(2,128)(2,1)S(1)}, u32[]{:S(2)}, u32[]{:S(2)}) async-start(bf16[32,2,384]{2,1,0:T(2,128)(2,1)} %reshape.227), calls=%async_computation.1 | async-start | bytes 98304 | tf_op jit(solution)/shard_map/all_to_all | solution.py:84
  86.1 25.2 %copy-start.9 = (bf16[2,4,32,2,32,1]{4,2,3,0,5,1:T(8,128)(2,1)S(1)}, bf16[2,4,32,2,32,1]{4,2,3,0,5,1:T(8,128)(2,1)}, u32[]{:S(2)}) copy-start(bf16[2,4,32,2,32,1]{4,2,3,0,5,1:T(8,128)(2,1)} %constant.37) | copy-start | bytes 98308
  118.2 18.0 %copy-start.1 = (bf16[1,24,32,16,128]{4,3,2,1,0:T(8,128)(2,1)S(1)}, bf16[1,24,32,16,128]{4,3,2,1,0:T(8,128)(2,1)}, u32[]{:S(2)}) copy-start(bf16[1,24,32,16,128]{4,3,2,1,0:T(8,128)(2,1)} %param.8) | copy-start | bytes 9437188
  130.1 25.7 %all-to-all-start.3 = ((bf16[32,24,512]{2,1,0:T(8,128)(2,1)}), bf16[32,24,512]{2,1,0:T(8,128)(2,1)}, u32[]{:S(2)}, u32[]{:S(2)}) async-start(bf16[32,24,512]{2,1,0:T(8,128)(2,1)} %reshape_reshape.22), calls=%async_computation.3 | async-start | bytes 1572864 | tf_op jit(solution)/shard_map/all_to_all | solution.py:74
  136.2 27.2 %copy-start.7 = (bf16[128,32,1,1]{0,1,3,2:T(8,128)(2,1)S(1)}, bf16[128,32,1,1]{0,1,3,2:T(8,128)(2,1)}, u32[]{:S(2)}) copy-start(bf16[128,32,1,1]{0,1,3,2:T(8,128)(2,1)} %constant.40) | copy-start | bytes 24580
  140.8 22.7 %copy-start.8 = (bf16[1,24,32,16,128]{4,3,2,1,0:T(8,128)(2,1)S(1)}, bf16[1,24,32,16,128]{4,3,2,1,0:T(8,128)(2,1)}, u32[]{:S(2)}) copy-start(bf16[1,24,32,16,128]{4,3,2,1,0:T(8,128)(2,1)} %param.9) | copy-start | bytes 9437188
  171.9 1.6 copy-start.2
  184.3 43.9 %copy-start.11 = (bf16[2,8,16,2,32,1,1]{4,2,0,1,3,5,6:T(8,128)(2,1)S(1)}, bf16[2,8,16,2,32,1,1]{4,2,0,1,3,5,6:T(8,128)(2,1)}, u32[]{:S(2)}) copy-start(bf16[2,8,16,2,32,1,1]{4,2,0,1,3,5,6:T(8,128)(2,1)} %constant.35) | copy-start | bytes 98308
  184.3 43.9 %copy-start.13 = (bf16[2,4,32,2,32,1]{4,2,0,1,3,5:T(8,128)(2,1)S(1)}, bf16[2,4,32,2,32,1]{4,2,0,1,3,5:T(8,128)(2,1)}, u32[]{:S(2)}) copy-start(bf16[2,4,32,2,32,1]{4,2,0,1,3,5:T(8,128)(2,1)} %constant.36) | copy-start | bytes 98308
  246.3 15.7 %copy-start.5 = (f32[32,16,24]{0,1,2:T(8,128)S(1)}, f32[32,16,24]{0,1,2:T(8,128)}, u32[]{:S(2)}) copy-start(f32[32,16,24]{0,1,2:T(8,128)} %get-tuple-element.35) | copy-start | bytes 147460
  246.4 15.8 %copy-start.4 = (f32[32,16,24]{0,1,2:T(8,128)S(1)}, f32[32,16,24]{0,1,2:T(8,128)}, u32[]{:S(2)}) copy-start(f32[32,16,24]{0,1,2:T(8,128)} %get-tuple-element.30) | copy-start | bytes 147460
  257.0 11.8 %all-to-all-start.6 = ((bf16[32,2,384]{2,1,0:T(2,128)(2,1)}), bf16[32,2,384]{2,1,0:T(2,128)(2,1)S(1)}, u32[]{:S(2)}, u32[]{:S(2)}) async-start(bf16[32,2,384]{2,1,0:T(2,128)(2,1)} %reshape.233), calls=%async_computation.6 | async-start | bytes 98304 | tf_op jit(solution)/shard_map/all_to_all | solution.py:89
  288.8 147.1 %all-to-all-start.7 = ((bf16[32,24,512]{2,1,0:T(8,128)(2,1)}), bf16[32,24,512]{2,1,0:T(8,128)(2,1)}, u32[]{:S(2)}, u32[]{:S(2)}) async-start(bf16[32,24,512]{2,1,0:T(8,128)(2,1)} %reshape_reshape.25), calls=%async_computation.7 | async-start | bytes 1572864 | tf_op jit(solution)/shard_map/all_to_all | solution.py:74
  294.4 137.3 %all-reduce.2.cloned.1.call-start = ((), (), s32[]{:S(2)}) async-start(), calls=%async_computation.8 | async-start | bytes 2621440 | tf_op jit(solution)/shard_map/psum | solution.py:124
  318.3 125.2 %copy-start.6 = (bf16[128,32,1,1]{0,1,3,2:T(8,128)(2,1)S(1)}, bf16[128,32,1,1]{0,1,3,2:T(8,128)(2,1)}, u32[]{:S(2)}) copy-start(bf16[128,32,1,1]{0,1,3,2:T(8,128)(2,1)} %constant.34) | copy-start | bytes 24580
Sparse Core Ops, SparseCore 0:
  311.9 119.7 all-reduce.1
where the time goes:
time: 468 us; the launch traced here: 459 us
  waiting for transfers between devices  133 us (28%)
  local copies, waits for them, and re-layouts  129 us (28%)
  blocking collectives  82.2 us (18%)
  matrix products  49.4 us (11%)
  other arithmetic  28.5 us (6%)
  starting transfers between devices  23.5 us (5%)
  between operations  14.7 us (3%)
    psum x1, waiting for transfers between devices, shards(): lax.psum(local_terms.astype(jnp.bfloat16), 'dp').astype(jnp.float32)  113 us
    all_to_all x2, blocking collectives, to_slab(): lax.all_to_all(merged, ('px', 'py'), split_axis=0, concat_axis=0, tiled=T...  55.1 us
    dot_general x10, matrix products, mixing(): return jnp.einsum(form, left, right, preferred_element_type=jnp.float32)  49.4 us
    another operation x2, local copies, waits for them, and re-layouts, to_pencil(): merged = blocks.reshape(devices_plane, group_size, block_cells)  23.6 us
    another operation x2, local copies, waits for them, and re-layouts, to_slab(): merged = blocks.reshape(devices_plane, group_size, block_cells)  22.2 us
    unnamed x4, other arithmetic  18 us
    another operation x6, local copies, waits for them, and re-layouts  17.9 us
    convert_element_type x2, local copies, waits for them, and re-layouts, to_modes(): lines = mixing('bcxyn,nq->bcqxy', source, table).astype(jnp.bfloat16)  15.3 us
  transfers between devices with their start and end apart: 5, of which 3 were waited for; matrix products, arithmetic and copies ran while one was open for 9% of the time, Pallas kernels for 0%

commit v1 on v0

v1 whole, which is shorter than its diff:
```python
import functools
import math

import jax
import jax.numpy as jnp
import ml_dtypes
import numpy as np
from jax import lax
from jax.experimental import pallas as pl
from jax.experimental.pallas import tpu as pltpu
from jax.sharding import PartitionSpec as P

MODES = 16
NX = 128
NY = 128
NZ = 128
CH = 24
PX = 4
PY = 8
DP = 8
XL = NX // PX
YL = NY // PY
CELLS = XL * YL
GROUPS = 3
GC = CH // GROUPS
LANES = GC * MODES
KX = 2 * MODES
KY = 2 * MODES
ROWS = 2 * KY
BLOCK = PY * 2 * YL
PIECE = 2 * YL
IO = CH * CH
MESH = pl.DeviceIdType.MESH
F32 = jnp.float32
BF16 = jnp.bfloat16


def bf(array):
    return np.asarray(array, np.float32).astype(ml_dtypes.bfloat16)


def axis_table(length, mode_count):
    grid_pos = np.arange(length)
    kept_freq = np.concatenate([np.arange(mode_count), np.arange(length - mode_count, length)])
    angles = 2.0 * math.pi * (kept_freq[None, :] * grid_pos[:, None] % length) / length
    norm_scale = length ** (-0.5)
    cosine = np.cos(angles) * norm_scale
    sine_part = np.sin(angles) * norm_scale
    result = np.zeros((2, length, 2, 2 * mode_count))
    result[0, :, 0, :] = cosine
    result[1, :, 0, :] = sine_part
    result[0, :, 1, :] = -sine_part
    result[1, :, 1, :] = cosine
    return result


def depth_tables(length, mode_count):
    grid_pos = np.arange(length)
    frequency = np.arange(mode_count)
    angles = 2.0 * math.pi * (frequency[None, :] * grid_pos[:, None] % length) / length
    norm_scale = length ** (-0.5)
    result = np.zeros((length, mode_count, 2))
    result[:, :, 0] = np.cos(angles) * norm_scale
    result[:, :, 1] = -np.sin(angles) * norm_scale
    doubling = np.where(frequency == 0, 1.0, 2.0)
    return result, result * doubling[None, :, None]


@functools.cache
def tables():
    plain, doubled = depth_tables(NZ, MODES)

    def depth(table):
        out = np.zeros((GC, NZ, 2, GC, MODES))
        for c in range(GC):
            out[c, :, :, c, :] = table.transpose(0, 2, 1)
        return out.reshape(GC * NZ, 2 * LANES)

    dz, dh = depth(plain), depth(doubled)
    cross = axis_table(NX, MODES).reshape(2, PX, XL, 2, KX)
    m1 = np.zeros((PX, KX, 2, YL, 2, XL, YL))
    for y in range(YL):
        m1[:, :, :, y, :, :, y] = cross.transpose(1, 4, 3, 0, 2)
    m1 = m1.reshape(PX, KX * 2 * YL, 2 * CELLS)
    along = axis_table(NY, MODES).reshape(2, PY, YL, 2, KY)
    my = along.transpose(3, 4, 1, 0, 2).reshape(ROWS, BLOCK)
    sel = np.zeros((CH, MODES, MODES, 128))
    for c in range(CH):
        for k in range(MODES):
            sel[c, k, k, c] = 1.0
    sel = sel.reshape(CH * MODES, MODES * 128)
    exp_i = np.zeros((128, CH, CH))
    exp_o = np.zeros((128, CH, CH))
    for c in range(CH):
        exp_i[c, c, :] = 1.0
        exp_o[c, :, c] = 1.0
    exp_i = exp_i.reshape(128, IO)
    exp_o = exp_o.reshape(128, IO)
    rep = np.zeros((CH * YL, CH))
    for c in range(CH):
        rep[c * YL : (c + 1) * YL, c] = 1.0
    return dict(
        dz=bf(dz), dh=bf(dh), dzt=bf(dz.T), dht=bf(dh.T),
        m1=bf(m1), m1t=bf(m1.transpose(0, 2, 1)),
        my=bf(my), myt=bf(my.T), sel=bf(sel), place=bf(sel.T),
        exp_i=bf(exp_i), exp_o=bf(exp_o), sum_i=bf(exp_i.T), sum_o=bf(exp_o.T),
        rep=bf(rep), rept=bf(rep.T),
    )


NAMES = (
    "dz", "m1", "rep", "rept", "my", "sel", "exp_i", "sum_o", "place", "myt", "m1t", "dht", "dh",
    "exp_o", "sum_i", "dzt",
)


def dot(a, b):
    return jnp.dot(a, b, preferred_element_type=F32)


def gelu_slope(values):
    normal_cdf = 0.5 * (1.0 + lax.erf(values * 0.7071067811865476))
    density = jnp.exp(-0.5 * values * values) * 0.3989422804014327
    return normal_cdf + values * density


def kernel(*refs):
    fields_h, cot_h, w_h, byp = refs[:4]
    tab_h = dict(zip(NAMES, refs[4 : 4 + len(NAMES)]))
    refs = refs[4 + len(NAMES) :]
    gw_h, gf_h = refs[:2]
    refs = refs[2:]
    tab = dict(zip(NAMES, refs[: len(NAMES)]))
    (
        fields, cot, gp, w, pb, out, bypk, bypkt, xbuf, tbuf, ybuf, rs, sbuf, rbuf, vbuf, ag, dpu, dpg,
        ue, ge, prod, us, gs, gw,
        load_sem, store_sem, rs_s, rs_r, a2_s, a2_r, ag_s, ag_r, dp_s, dp_r,
    ) = refs[len(NAMES) :]

    px = lax.axis_index("px")
    py = lax.axis_index("py")
    dp = lax.axis_index("dp")
    zhi = dp // 4
    yy = lax.rem(dp, 4)

    loads = {}

    def load(name, src, dst, index):
        copy = pltpu.make_async_copy(src, dst, load_sem.at[index])
        copy.start()
        loads[name] = copy

    load("f0", fields_h.at[pl.ds(0, GC)], fields.at[pl.ds(0, GC)], 0)
    load("dz", tab_h["dz"], tab["dz"], 1)
    load("m1", tab_h["m1"].at[px], tab["m1"], 2)
    load("f1", fields_h.at[pl.ds(GC, GC)], fields.at[pl.ds(GC, GC)], 3)
    load("f2", fields_h.at[pl.ds(2 * GC, GC)], fields.at[pl.ds(2 * GC, GC)], 4)
    load("w", w_h, w, 5)
    index = 6
    for name in NAMES[2:]:
        src = tab_h[name].at[px] if name == "m1t" else tab_h[name]
        load(name, src, tab[name], index)
        index += 1
    load("cot", cot_h, cot, index)
    waited = set()

    def need(*names):
        for name in names:
            if name not in waited:
                loads[name].wait()
                waited.add(name)

    def at_px(j):
        return {"px": lax.rem(px + j, PX)}

    def at_py(k):
        return {"py": lax.rem(py + k, PY)}

    def at_y(j):
        return {"dp": zhi * 4 + lax.rem(yy + j, 4)}

    far = {"dp": lax.rem(dp + 4, DP)}
    partners = [at_px(j) for j in range(1, PX)] + [at_py(k) for k in range(1, PY)]
    partners += [at_y(j) for j in range(1, 4)] + [far]
    barrier = pltpu.get_barrier_semaphore()
    for where in partners:
        pl.semaphore_signal(barrier, inc=1, device_id=where, device_id_type=MESH)

    sends = []

    def send(src, dst, send_sem, recv_sem, where):
        copy = pltpu.make_async_remote_copy(
            src_ref=src, dst_ref=dst, send_sem=send_sem, recv_sem=recv_sem,
            device_id=where, device_id_type=MESH,
        )
        copy.start()
        sends.append(copy)
        return copy

    rs_c, a2_c, ag_c, dp_c = {}, {}, {}, {}

    def cross_and_send(t, g):
        for j in (2, 1, 3, 0):
            dest = lax.rem(px + j, PX)
            rows = pl.ds(pl.multiple_of(dest * BLOCK, BLOCK), BLOCK)
            ybuf[t, g, rows, :] = dot(tab["m1"][rows, :], xbuf[...]).astype(BF16)
            if j:
                rs_c[t, g, j] = send(
                    ybuf.at[t, g, rows], rs.at[t, g, j - 1], rs_s.at[t, g, j - 1], rs_r.at[t, g, j - 1], at_px(j)
                )

    def depth_rows(r, lhs, table):
        part = dot(lhs, table).astype(BF16)
        n = lhs.shape[0]
        xbuf[pl.ds(pl.multiple_of(r * n, n), n), :] = part[:, :LANES]
        xbuf[pl.ds(pl.multiple_of(CELLS + r * n, n), n), :] = part[:, LANES:]

    def reduce_and_send(t, g):
        for j in range(1, PX):
            rs_c[t, g, j].wait_recv()
        own = pl.ds(pl.multiple_of(px * BLOCK, BLOCK), BLOCK)
        total = ybuf[t, g, own, :].astype(F32)
        for j in range(1, PX):
            total = total + rs[t, g, j - 1].astype(F32)
        sbuf[t, g] = total.astype(BF16)
        mine = pl.ds(pl.multiple_of(py * PIECE, PIECE), PIECE)
        for k in range(1, PY):
            dest = lax.rem(py + k, PY)
            rows = pl.ds(pl.multiple_of(dest * PIECE, PIECE), PIECE)
            a2_c[2 * t, g, k] = send(
                sbuf.at[t, g, rows], rbuf.at[t, g, mine], a2_s.at[2 * t, g, k - 1], a2_r.at[2 * t, g, k - 1], at_py(k)
            )
        rbuf[t, g, mine, :] = sbuf[t, g, mine, :]

    def spectrum(t):
        for g in range(GROUPS):
            for k in range(1, PY):
                a2_c[2 * t, g, k].wait_recv()
        lines = jnp.concatenate([rbuf[t, g] for g in range(GROUPS)], axis=1)
        return dot(tab["my"][...], lines).astype(BF16)

    def spread(hat, sel_to, expand, target):
        chosen = dot(hat, tab["sel"][...]).astype(BF16)
        for k in range(MODES):
            sel_to[pl.ds(k * ROWS, ROWS), :] = chosen[:, k * 128 : (k + 1) * 128]

        def body(b, _):
            rows = pl.ds(pl.multiple_of(b * 256, 256), 256)
            target[rows, :] = dot(sel_to[rows, :], expand[...]).astype(BF16)
            return 0

        lax.fori_loop(0, 4, body, 0)

    def mix(target, conj, collapse):
        def body(k, _):
            re = pl.ds(pl.multiple_of(k * ROWS, ROWS), KY)
            im = pl.ds(pl.multiple_of(k * ROWS + KY, KY), KY)
            w_re, w_im = w[re, :].astype(F32), w[im, :].astype(F32)
            u_re, u_im = target[re, :].astype(F32), target[im, :].astype(F32)
            if conj:
                prod[re, :] = (w_re * u_re + w_im * u_im).astype(BF16)
                prod[im, :] = (w_re * u_im - w_im * u_re).astype(BF16)
            else:
                prod[re, :] = (w_re * u_re - w_im * u_im).astype(BF16)
                prod[im, :] = (w_re * u_im + w_im * u_re).astype(BF16)
            return 0

        lax.fori_loop(0, MODES, body, 0)
        summed = dot(prod[...], collapse[...]).astype(BF16)
        wide = jnp.concatenate([summed[k * ROWS : (k + 1) * ROWS] for k in range(MODES)], axis=1)
        return dot(wide, tab["place"][...]).astype(BF16)

    own_block = pl.ds(pl.multiple_of(px * BLOCK, BLOCK), BLOCK)

    def inverse_send(t, mixed):
        lines = dot(tab["myt"][...], mixed).astype(BF16)
        mine = pl.ds(pl.multiple_of(px * BLOCK + py * PIECE, PIECE), PIECE)
        for g in range(GROUPS):
            vbuf[t, g] = lines[:, g * LANES : (g + 1) * LANES]
            for k in range(1, PY):
                dest = lax.rem(py + k, PY)
                rows = pl.ds(pl.multiple_of(dest * PIECE, PIECE), PIECE)
                a2_c[2 * t + 1, g, k] = send(
                    vbuf.at[t, g, rows], ag.at[t, g, mine],
                    a2_s.at[2 * t + 1, g, k - 1], a2_r.at[2 * t + 1, g, k - 1], at_py(k),
                )
            here = pl.ds(pl.multiple_of(py * PIECE, PIECE), PIECE)
            ag[t, g, mine, :] = vbuf[t, g, here, :]

    def gather_send(t, g):
        for k in range(1, PY):
            a2_c[2 * t + 1, g, k].wait_recv()
        for j in (2, 1, 3):
            ag_c[t, g, j] = send(
                ag.at[t, g, own_block], ag.at[t, g, own_block], ag_s.at[t, g, j - 1], ag_r.at[t, g, j - 1], at_px(j)
            )

    def cross_back(t, g):
        for j in range(1, PX):
            ag_c[t, g, j].wait_recv()

        def body(b, _):
            rows = pl.ds(pl.multiple_of(b * 256, 256), 256)
            tbuf[rows, :] = dot(tab["m1t"][rows, :], ag[t, g]).astype(BF16)
            return 0

        lax.fori_loop(0, 4, body, 0)

    CHUNK = 128

    def field_values(r, table):
        rows = pl.ds(pl.multiple_of(r * CHUNK, CHUNK), CHUNK)
        rows_im = pl.ds(pl.multiple_of(CELLS + r * CHUNK, CHUNK), CHUNK)
        return dot(jnp.concatenate([tbuf[rows, :], tbuf[rows_im, :]], axis=1), table)

    def bypass_all(matrix, source):
        def body(b, _):
            parts = []
            for e in range(2):
                rows = pl.ds(pl.multiple_of(b * 32 + e * 16, 16), 16)
                parts.append(source[:, rows, :].reshape(CH * YL, NZ))
            value = dot(matrix[...], jnp.concatenate(parts, axis=1))
            for e in range(2):
                rows = pl.ds(pl.multiple_of(b * 32 + e * 16, 16), 16)
                pb[:, rows, :] = value[:, e * NZ : (e + 1) * NZ].reshape(CH, YL, NZ)
            return 0

        lax.fori_loop(0, CELLS // 32, body, 0)

    need("f0", "dz", "m1")
    for g in range(GROUPS):
        need("f%d" % g)

        def body(r, _):
            rows = pl.ds(pl.multiple_of(r * 256, 256), 256)
            lhs = jnp.concatenate([fields[g * GC + c, rows, :] for c in range(GC)], axis=1)
            depth_rows(r, lhs, tab["dz"][...])
            return 0

        lax.fori_loop(0, 2, body, 0)
        if g == 0:
            pl.semaphore_wait(barrier, len(partners))
        cross_and_send(0, g)

    need("rep", "rept")
    mask = lax.rem(lax.broadcasted_iota(jnp.int32, (CH * YL, CH * YL), 0), YL) == lax.rem(
        lax.broadcasted_iota(jnp.int32, (CH * YL, CH * YL), 1), YL
    )
    left = dot(tab["rep"][...], byp[...]).astype(BF16)
    full = dot(left, tab["rept"][...])
    bypk[...] = jnp.where(mask, full, 0.0).astype(BF16)
    bypkt[...] = jnp.where(mask, full, 0.0).T.astype(BF16)

    reduce_and_send(0, 0)
    reduce_and_send(0, 1)
    bypass_all(bypk, fields)
    reduce_and_send(0, 2)

    need("my", "sel", "exp_i", "sum_o", "place", "myt", "w")
    u_hat = spectrum(0)
    dpu[0] = u_hat
    dp_c["u", 0] = send(dpu.at[0], dpu.at[1], dp_s.at[0, 0], dp_r.at[0, 0], far)
    spread(u_hat, us, tab["exp_i"], ue)
    inverse_send(0, mix(ue, False, tab["sum_o"]))
    need("m1t", "dht", "dh", "cot")
    for g in range(GROUPS):
        gather_send(0, g)
    dp_c["u", 0].wait_recv()
    for j in range(1, 4):
        dp_c["u", j] = send(dpu.at[pl.ds(0, 2)], dpu.at[pl.ds(2 * j, 2)], dp_s.at[0, j], dp_r.at[0, j], at_y(j))

    for g in range(GROUPS):
        cross_back(0, g)

        def body(r, _):
            values = field_values(r, tab["dht"][...])
            rows = pl.ds(pl.multiple_of(r * CHUNK, CHUNK), CHUNK)
            parts = []
            for c in range(GC):
                pre = values[:, c * NZ : (c + 1) * NZ] + pb[g * GC + c, rows, :]
                slope = gelu_slope(pre)
                part = (cot[g * GC + c, rows, :].astype(F32) * slope).astype(BF16)
                gp[g * GC + c, rows, :] = part
                parts.append(part)
            depth_rows(r, jnp.concatenate(parts, axis=1), tab["dh"][...])
            return 0

        lax.fori_loop(0, CELLS // CHUNK, body, 0)
        cross_and_send(1, g)
        if g:
            reduce_and_send(1, g - 1)
    bypass_all(bypkt, gp)
    reduce_and_send(1, GROUPS - 1)

    need("exp_o", "sum_i", "dzt")
    g_hat = spectrum(1)
    dpg[0] = g_hat
    dp_c["g", 0] = send(dpg.at[0], dpg.at[1], dp_s.at[1, 0], dp_r.at[1, 0], far)
    spread(g_hat, us, tab["exp_o"], ge)
    inverse_send(1, mix(ge, True, tab["sum_i"]))
    for g in range(GROUPS):
        gather_send(1, g)
    dp_c["g", 0].wait_recv()
    for j in range(1, 4):
        dp_c["g", j] = send(dpg.at[pl.ds(0, 2)], dpg.at[pl.ds(2 * j, 2)], dp_s.at[1, j], dp_r.at[1, j], at_y(j))

    def choose(source, target):
        rows_all = source[...].reshape(DP * ROWS, CH * MODES)
        for b in range(MODES // 2):
            cols = slice(b * 256, (b + 1) * 256)
            chosen = dot(rows_all, tab["sel"][:, cols]).astype(BF16)
            target[2 * b] = chosen[:, :128]
            target[2 * b + 1] = chosen[:, 128:]

    for j in range(1, 4):
        dp_c["u", j].wait_recv()
    choose(dpu, gs.at[0])
    for j in range(1, 4):
        dp_c["g", j].wait_recv()
    choose(dpg, gs.at[1])

    def gw_body(k, _):
        u_all = dot(gs[0, k], tab["exp_i"][...])
        g_all = dot(gs[1, k], tab["exp_o"][...])
        real = jnp.zeros((KY, IO), F32)
        imag = jnp.zeros((KY, IO), F32)
        for d in range(DP):
            u_re, u_im = u_all[d * ROWS : d * ROWS + KY], u_all[d * ROWS + KY : (d + 1) * ROWS]
            g_re, g_im = g_all[d * ROWS : d * ROWS + KY], g_all[d * ROWS + KY : (d + 1) * ROWS]
            real += g_re * u_re + g_im * u_im
            imag += g_im * u_re - g_re * u_im
        gw[pl.ds(pl.multiple_of(k * ROWS, ROWS), KY), :] = real
        gw[pl.ds(pl.multiple_of(k * ROWS + KY, KY), KY), :] = imag
        return 0

    lax.fori_loop(0, MODES, gw_body, 0)
    stores = [pltpu.make_async_copy(gw, gw_h, store_sem.at[GROUPS])]
    stores[0].start()

    for g in range(GROUPS):
        cross_back(1, g)

        def body(r, _):
            values = field_values(r, tab["dzt"][...])
            rows = pl.ds(pl.multiple_of(r * CHUNK, CHUNK), CHUNK)
            for c in range(GC):
                total = values[:, c * NZ : (c + 1) * NZ] + pb[g * GC + c, rows, :]
                out[g * GC + c, rows, :] = total.astype(BF16)
            return 0

        lax.fori_loop(0, CELLS // CHUNK, body, 0)
        part = pl.ds(g * GC, GC)
        copy = pltpu.make_async_copy(out.at[part], gf_h.at[part], store_sem.at[g])
        copy.start()
        stores.append(copy)

    for copy in stores:
        copy.wait()
    for copy in sends:
        copy.wait_send()


def shards(fields, cotangent, spectral_weight, bypass):
    tab = tables()
    arrays = [jnp.asarray(tab[name]) for name in NAMES]
    w = spectral_weight.transpose(1, 2, 0, 3).reshape(MODES * ROWS, IO)
    any_spec = pl.BlockSpec(memory_space=pl.ANY)
    vmem = pltpu.VMEM
    shapes = [a.shape[1:] if name in ("m1", "m1t") else a.shape for name, a in zip(NAMES, arrays)]
    scratch = [vmem(shape, BF16) for shape in shapes] + [
        vmem((CH, CELLS, NZ), BF16),
        vmem((CH, CELLS, NZ), BF16),
        vmem((CH, CELLS, NZ), BF16),
        vmem((MODES * ROWS, IO), BF16),
        vmem((CH, CELLS, NZ), F32),
        vmem((CH, CELLS, NZ), BF16),
        vmem((CH * YL, CH * YL), BF16),
        vmem((CH * YL, CH * YL), BF16),
        vmem((2 * CELLS, LANES), BF16),
        vmem((2 * CELLS, LANES), BF16),
        vmem((2, GROUPS, PX * BLOCK, LANES), BF16),
        vmem((2, GROUPS, PX - 1, BLOCK, LANES), BF16),
        vmem((2, GROUPS, BLOCK, LANES), BF16),
        vmem((2, GROUPS, BLOCK, LANES), BF16),
        vmem((2, GROUPS, BLOCK, LANES), BF16),
        vmem((2, GROUPS, PX * BLOCK, LANES), BF16),
        vmem((DP, ROWS, CH * MODES), BF16),
        vmem((DP, ROWS, CH * MODES), BF16),
        vmem((MODES * ROWS, IO), BF16),
        vmem((MODES * ROWS, IO), BF16),
        vmem((MODES * ROWS, IO), BF16),
        vmem((MODES * ROWS, 128), BF16),
        vmem((2, MODES, DP * ROWS, 128), BF16),
        vmem((MODES * ROWS, IO), F32),
        pltpu.SemaphoreType.DMA((len(NAMES) + 5,)),
        pltpu.SemaphoreType.DMA((GROUPS + 1,)),
        pltpu.SemaphoreType.DMA((2, GROUPS, PX - 1)),
        pltpu.SemaphoreType.DMA((2, GROUPS, PX - 1)),
        pltpu.SemaphoreType.DMA((4, GROUPS, PY - 1)),
        pltpu.SemaphoreType.DMA((4, GROUPS, PY - 1)),
        pltpu.SemaphoreType.DMA((2, GROUPS, PX - 1)),
        pltpu.SemaphoreType.DMA((2, GROUPS, PX - 1)),
        pltpu.SemaphoreType.DMA((2, 4)),
        pltpu.SemaphoreType.DMA((2, 4)),
    ]
    gw, gf = pl.pallas_call(
        kernel,
        out_shape=(
            jax.ShapeDtypeStruct((MODES * ROWS, IO), F32),
            jax.ShapeDtypeStruct((CH, CELLS, NZ), BF16),
        ),
        in_specs=[any_spec] * 3 + [pl.BlockSpec(memory_space=pltpu.VMEM)] + [any_spec] * len(arrays),
        out_specs=(any_spec, any_spec),
        scratch_shapes=scratch,
        compiler_params=pltpu.CompilerParams(
            collective_id=0, has_side_effects=True, vmem_limit_bytes=60 * 1024 * 1024
        ),
        cost_estimate=pl.CostEstimate(flops=20_000_000_000, bytes_accessed=30_000_000, transcendentals=3_000_000),
    )(
        fields.reshape(CH, CELLS, NZ), cotangent.reshape(CH, CELLS, NZ), w, bypass, *arrays
    )
    grad_weight = gw.reshape(MODES, 2, KY, IO).transpose(2, 0, 1, 3)
    return grad_weight, gf.reshape(1, CH, XL, YL, NZ)


def solution(mesh):
    in_specs = (
        P("dp", None, "px", "py", None),
        P("dp", None, "px", "py", None),
        P(("px", "py"), None, None, None),
        P(),
    )
    out_specs = (P(("px", "py"), None, None, None), P("dp", None, "px", "py", None))
    return jax.shard_map(shards, mesh=mesh, in_specs=in_specs, out_specs=out_specs, check_vma=False)
```

time: 468 us -> 109 us (0.23); the launches traced: 459 us -> 107 us
  waiting for transfers between devices: 133 us -> 0 us
  local copies, waits for them, and re-layouts: 129 us -> 9.86 us
  Pallas kernels: 0 us -> 96.8 us
  blocking collectives: 82.2 us -> 0 us
  matrix products: 49.4 us -> 0 us
  other arithmetic: 28.5 us -> 0 us
  starting transfers between devices: 23.5 us -> 0 us
  between operations: 14.7 us -> 0.65 us
    psum x1 -> x0, waiting for transfers between devices: 113 us -> none  [shards(): lax.psum(local_terms.astype(jnp.bfloat16), 'dp').astype(jnp.float32)]
    pallas_call x0 -> x1, Pallas kernels: none -> 96.8 us  [shards(): pl.pallas_call(kernel, out_shape=(jax.ShapeDtypeStruct((MODES * ROWS, IO)...]
    another operation x16 -> x0, local copies, waits for them, and re-layouts: 84.5 us -> none  [the longest x2 23.6 us: to_pencil(): merged = blocks.reshape(devices_plane, group_size, block_cells)]
    all_to_all x4 -> x0, blocking collectives: 82.2 us -> none  [the longest x2 55.1 us: to_slab(): lax.all_to_all(merged, ('px', 'py'), split_axis=0, concat_axis=0, tiled=T...]
    dot_general x10 -> x0, matrix products: 49.4 us -> none  [mixing(): return jnp.einsum(form, left, right, preferred_element_type=jnp.float32)]
    convert_element_type x4 -> x0, local copies, waits for them, and re-layouts: 24.9 us -> none  [the longest x2 15.3 us: to_modes(): lines = mixing('bcxyn,nq->bcqxy', source, table).astype(jnp.bfloat16)]
    all_to_all x4 -> x0, starting transfers between devices: 23.3 us -> none  [the longest x2 11.7 us: to_pencil(): lax.all_to_all(merged, ('px', 'py'), split_axis=0, concat_axis=0, tiled=T...]
    all_to_all x4 -> x0, waiting for transfers between devices: 19.1 us -> none  [the longest x2 15.1 us: to_pencil(): lax.all_to_all(merged, ('px', 'py'), split_axis=0, concat_axis=0, tiled=T...]
  transfers between devices with their start and end apart: 5 -> 0, of which waited for: 3 -> 0; matrix products, arithmetic and copies ran while one was open for 9% -> 0% of each run, Pallas kernels for 0% -> 0%
where the time goes in v1:
time: 109 us; the launch traced here: 107 us
  Pallas kernels  96.8 us (89%)
  local copies, waits for them, and re-layouts  9.86 us (9%)
    pallas_call x1, Pallas kernels, shards(): pl.pallas_call(kernel, out_shape=(jax.ShapeDtypeStruct((MODES * ROWS, IO)...  96.8 us
    reshape x1, local copies, waits for them, and re-layouts, shards(): grad_weight = gw.reshape(MODES, 2, KY, IO).transpose(2, 0, 1, 3)  5.4 us
    transpose x1, local copies, waits for them, and re-layouts, shards(): w = spectral_weight.transpose(1, 2, 0, 3).reshape(MODES * ROWS, IO)  2.78 us

profile of v1, /device:TPU:2, one launch (start us, length us, event | category | flops | bytes accessed | tf_op | source)
XLA Modules:
  0.0 107.3 jit_solution(6289045816245686268)
XLA Ops:
  0.6 2.8 %copy.22 = bf16[16,2,32,576]{3,2,1,0:T(8,128)(2,1)} copy(bf16[16,2,32,576]{3,1,0,2:T(2,128)(2,1)} %bitcast.12) | data formatting | bytes 2359296 | tf_op jit(solution)/shard_map/transpose | solution.py:466
  3.4 96.8 %shard_map.203 = (f32[1024,576]{1,0:T(8,128)}, bf16[24,512,128]{2,1,0:T(8,128)(2,1)}) custom-call(bf16[24,512,128]{2,1,0:T(8,128)(2,1)} %bitcast.14, bf16[24,512,128]{2,1,0:T(8,128)(2,1)} %bitcast.15, bf16[1024,576]{1,0:T(8,128)(2,1)} %bitcast.13, bf16[24,24]{1,0:T(8,128)(2,1)} %refs_3_.1, bf16[1024,256]{1,0:T(8,128)(2,1)} %constant.32.clone.refs_4_, ...), custom_call_target="tpu_custom_call" | custom-call | flops 20000000000 | bytes 30000000 | tf_op jit(solution)/shard_map/pallas_call | solution.py:506
  100.2 0.0 copy-start
  100.2 5.4 %copy.25 = f32[16,2,32,576]{3,1,0,2:T(2,128)} copy(f32[16,2,32,576]{3,2,1,0:T(8,128)} %bitcast.10) | data formatting | bytes 4718592 | tf_op jit(solution)/shard_map/reshape | solution.py:522
  105.6 0.0 copy-done
  105.6 1.7 %copy.27 = bf16[1,24,32,16,128]{4,3,2,1,0:T(8,128)(2,1)} copy(bf16[1,24,32,16,128]{4,3,2,1,0:T(8,128)(2,1)S(1)} %bitcast.9) | data formatting | bytes 6291456
Async XLA Ops:
  100.2 5.4 %copy-start = (bf16[24,512,128]{2,1,0:T(8,128)(2,1)S(1)}, bf16[24,512,128]{2,1,0:T(8,128)(2,1)}, u32[]{:S(2)}) copy-start(bf16[24,512,128]{2,1,0:T(8,128)(2,1)} %get-tuple-element.5) | copy-start | bytes 9437188

commit v2 on v1

v2 whole, which is shorter than its diff:
```python
import functools
import math

import jax
import jax.numpy as jnp
import ml_dtypes
import numpy as np
from jax import lax
from jax.experimental import pallas as pl
from jax.experimental.pallas import tpu as pltpu
from jax.sharding import PartitionSpec as P

MODES = 16
NX = 128
NY = 128
NZ = 128
CH = 24
PX = 4
PY = 8
DP = 8
XL = NX // PX
YL = NY // PY
CELLS = XL * YL
GROUPS = 3
GC = CH // GROUPS
LANES = GC * MODES
KX = 2 * MODES
KY = 2 * MODES
ROWS = 2 * KY
BLOCK = PY * 2 * YL
PIECE = 2 * YL
IO = CH * CH
WIDE = 640
PATTERN = 384
ORDER = (2, 1, 3, 0)
HALF = MODES // 2
XROWS = 2 * PY
YLANES = YL * LANES
NEAR = DP // 2
CHUNK = 128
MESH = pl.DeviceIdType.MESH
F32 = jnp.float32
BF16 = jnp.bfloat16


def bf(array):
    return np.asarray(array, np.float32).astype(ml_dtypes.bfloat16)


def axis_table(length, mode_count):
    grid_pos = np.arange(length)
    kept_freq = np.concatenate([np.arange(mode_count), np.arange(length - mode_count, length)])
    angles = 2.0 * math.pi * (kept_freq[None, :] * grid_pos[:, None] % length) / length
    norm_scale = length ** (-0.5)
    cosine = np.cos(angles) * norm_scale
    sine_part = np.sin(angles) * norm_scale
    result = np.zeros((2, length, 2, 2 * mode_count))
    result[0, :, 0, :] = cosine
    result[1, :, 0, :] = sine_part
    result[0, :, 1, :] = -sine_part
    result[1, :, 1, :] = cosine
    return result


def depth_tables(length, mode_count):
    grid_pos = np.arange(length)
    frequency = np.arange(mode_count)
    angles = 2.0 * math.pi * (frequency[None, :] * grid_pos[:, None] % length) / length
    norm_scale = length ** (-0.5)
    result = np.zeros((length, mode_count, 2))
    result[:, :, 0] = np.cos(angles) * norm_scale
    result[:, :, 1] = -np.sin(angles) * norm_scale
    doubling = np.where(frequency == 0, 1.0, 2.0)
    return result, result * doubling[None, :, None]


@functools.cache
def tables():
    plain, doubled = depth_tables(NZ, MODES)

    def depth(table):
        out = np.zeros((GC, NZ, 2, GC, MODES))
        for c in range(GC):
            out[c, :, :, c, :] = table.transpose(0, 2, 1)
        return out.reshape(GC * NZ, 2 * LANES)

    dz, dh = depth(plain), depth(doubled)
    cross = axis_table(NX, MODES).reshape(2, PX, XL, 2, KX)
    m1 = cross.transpose(1, 4, 3, 0, 2).reshape(PX, KX * 2, 2 * XL)
    along = axis_table(NY, MODES).reshape(2, PY, YL, 2, KY)
    my = along.transpose(3, 4, 1, 0, 2).reshape(ROWS, BLOCK)
    sel = np.zeros((2, CH, MODES, MODES, 2, 32))
    for c in range(CH):
        for k in range(MODES):
            sel[0, c, k, k, 0, c] = 1.0
            sel[1, c, k, k, 1, c] = 1.0
    sel = sel.reshape(2 * CH * MODES, MODES * 64)
    exp_i = np.zeros((CH, CH, CH))
    exp_o = np.zeros((CH, CH, CH))
    for c in range(CH):
        exp_i[c, c, :] = 1.0
        exp_o[c, :, c] = 1.0
    exp_i = exp_i.reshape(CH, IO)
    exp_o = exp_o.reshape(CH, IO)
    expand = np.zeros((2, 2, 64, WIDE + PATTERN))
    sum_i = np.zeros((2, IO, 2, 64))
    sum_o = np.zeros((2, IO, 2, 64))
    for q in range(2):
        expand[q, q, :CH, :IO] = exp_i
        expand[q, q, 32 : 32 + CH, WIDE:] = exp_o[:, :PATTERN]
        sum_i[q, :, q, :CH] = exp_i.T
        sum_o[q, :, q, :CH] = exp_o.T
    expand = expand.reshape(2, 128, WIDE + PATTERN)
    sum_i = sum_i.reshape(2, IO, 128)
    sum_o = sum_o.reshape(2, IO, 128)
    turned = np.stack([
        m1[p].reshape(PX, XROWS, 2 * XL)[[(p + j) % PX for j in ORDER]].reshape(PX * XROWS, 2 * XL)
        for p in range(PX)
    ])
    rep = np.zeros((CH * YL, CH))
    for c in range(CH):
        rep[c * YL : (c + 1) * YL, c] = 1.0
    return dict(
        dz=bf(dz), dh=bf(dh), dzt=bf(dz.T), dht=bf(dh.T),
        m1=bf(turned), m1t=bf(m1.transpose(0, 2, 1)),
        my=bf(my), myt=bf(my.T), sel=bf(sel), place=bf(sel[: CH * MODES].T),
        expand=bf(expand), sum_i=bf(sum_i), sum_o=bf(sum_o),
        rep=bf(rep), rept=bf(rep.T),
    )


NAMES = (
    "dz", "m1", "m1t", "rep", "rept", "my", "sel", "expand", "sum_o", "place", "myt", "dht", "dh",
    "sum_i", "dzt",
)


def dot(a, b):
    return jnp.dot(a, b, preferred_element_type=F32)


def gelu_slope(values):
    normal_cdf = 0.5 * (1.0 + lax.erf(values * 0.7071067811865476))
    density = jnp.exp(-0.5 * values * values) * 0.3989422804014327
    return normal_cdf + values * density


def kernel(*refs):
    fields_h, cot_h, w_h, byp = refs[:4]
    tab_h = dict(zip(NAMES, refs[4 : 4 + len(NAMES)]))
    refs = refs[4 + len(NAMES) :]
    gw_h, gf_h = refs[:2]
    refs = refs[2:]
    tab = dict(zip(NAMES, refs[: len(NAMES)]))
    (
        fields, cot, gp, w4, w, pb, out, bypk, bypkt, xbuf, tbuf, zval, lines, turn, back, wide_ag, ybuf, rs, sbuf, rbuf, vbuf, ag, dpu, dpg,
        ue, prod, us, gs, wide, acc, gw,
        load_sem, store_sem, rs_s, rs_r, a2_s, a2_r, ag_s, ag_r, dp_s, dp_r,
    ) = refs[len(NAMES) :]

    px = lax.axis_index("px")
    py = lax.axis_index("py")
    dp = lax.axis_index("dp")
    zhi = dp // 4
    yy = lax.rem(dp, 4)

    loads = {}

    def load(name, src, dst, index):
        copy = pltpu.make_async_copy(src, dst, load_sem.at[index])
        copy.start()
        loads[name] = copy

    def load_later():
        for index, name in enumerate(NAMES[3:]):
            load(name, tab_h[name], tab[name], 7 + index)
        load("cot", cot_h, cot, 7 + len(NAMES) - 3)

    load("f0", fields_h.at[pl.ds(0, GC)], fields.at[pl.ds(0, GC)], 0)
    load("dz", tab_h["dz"], tab["dz"], 1)
    load("m1", tab_h["m1"].at[px], tab["m1"], 2)
    waited = set()

    def need(*names):
        for name in names:
            if name not in waited:
                loads[name].wait()
                waited.add(name)

    def at_px(j):
        return {"px": lax.rem(px + j, PX)}

    def at_py(k):
        return {"py": lax.rem(py + k, PY)}

    def at_y(j):
        return {"dp": zhi * 4 + lax.rem(yy + j, 4)}

    far = {"dp": lax.rem(dp + 4, DP)}
    partners = [at_px(j) for j in range(1, PX)] + [at_py(k) for k in range(1, PY)]
    partners += [at_y(j) for j in range(1, 4)] + [far]
    barrier = pltpu.get_barrier_semaphore()
    for where in partners:
        pl.semaphore_signal(barrier, inc=1, device_id=where, device_id_type=MESH)

    sends = []

    def send(src, dst, send_sem, recv_sem, where):
        copy = pltpu.make_async_remote_copy(
            src_ref=src, dst_ref=dst, send_sem=send_sem, recv_sem=recv_sem,
            device_id=where, device_id_type=MESH,
        )
        copy.start()
        sends.append(copy)
        return copy

    rs_c, a2_c, ag_c, dp_c = {}, {}, {}, {}

    def cross_and_send(t, g):
        made = dot(tab["m1"][...], xbuf[...]).astype(BF16)
        for pos, j in enumerate(ORDER):
            ybuf[t, g, pos] = made[pos * XROWS : (pos + 1) * XROWS]
            if j:
                rs_c[t, g, j] = send(
                    ybuf.at[t, g, pos], rs.at[t, g, j - 1], rs_s.at[t, g, j - 1], rs_r.at[t, g, j - 1], at_px(j)
                )

    def depth(source, g, table):
        lhs = jnp.concatenate([source[g * GC + c] for c in range(GC)], axis=1)
        part = dot(lhs, table[...])
        for s in range(2):
            lines[s] = part[:, s * LANES : (s + 1) * LANES]
        for y in range(YL):
            for s in range(2):
                xbuf[s * XL : (s + 1) * XL, y * LANES : (y + 1) * LANES] = lines[
                    s, pl.ds(y, XL, stride=YL), :
                ].astype(BF16)

    def reduce_and_send(t, g):
        for j in range(1, PX):
            rs_c[t, g, j].wait_recv()
        total = ybuf[t, g, ORDER.index(0)].astype(F32)
        for j in range(1, PX):
            total = total + rs[t, g, j - 1].astype(F32)
        for y in range(YL):
            turn[y * XROWS : (y + 1) * XROWS, :] = total[:, y * LANES : (y + 1) * LANES]
        for r in range(XROWS):
            sbuf[t, g, r * YL : (r + 1) * YL, :] = turn[pl.ds(r, YL, stride=XROWS), :].astype(BF16)
        mine = pl.ds(pl.multiple_of(py * PIECE, PIECE), PIECE)
        for k in range(1, PY):
            dest = lax.rem(py + k, PY)
            rows = pl.ds(pl.multiple_of(dest * PIECE, PIECE), PIECE)
            a2_c[2 * t, g, k] = send(
                sbuf.at[t, g, rows], rbuf.at[t, g, mine], a2_s.at[2 * t, g, k - 1], a2_r.at[2 * t, g, k - 1], at_py(k)
            )
        rbuf[t, g, mine, :] = sbuf[t, g, mine, :]

    def spectrum(t):
        for g in range(GROUPS):
            for k in range(1, PY):
                a2_c[2 * t, g, k].wait_recv()
        rows = jnp.concatenate([rbuf[t, g] for g in range(GROUPS)], axis=1)
        return dot(tab["my"][...], rows).astype(BF16)

    def spread(hat, which):
        part = slice(which * CH * MODES, (which + 1) * CH * MODES)
        chosen = dot(hat, tab["sel"][part, :]).astype(BF16)
        for b in range(HALF):
            us[b * ROWS : (b + 1) * ROWS, :] = chosen[:, b * 128 : (b + 1) * 128]
        for q in range(2):
            if which:
                ue[q, :, :PATTERN] = dot(us[...], tab["expand"][q, :, WIDE:]).astype(BF16)
            else:
                ue[q] = dot(us[...], tab["expand"][q, :, :WIDE]).astype(BF16)

    def mix(which, collapse):
        def body(n, _):
            q, b = n // HALF, lax.rem(n, HALF)
            re = pl.ds(pl.multiple_of(b * ROWS, ROWS), KY)
            im = pl.ds(pl.multiple_of(b * ROWS + KY, KY), KY)
            for v in range(WIDE // 128):
                cols = slice(v * 128, min((v + 1) * 128, IO))
                size = cols.stop - cols.start
                at = (v % 3) * 128 if which else v * 128
                w_re, w_im = w[q, re, cols].astype(F32), w[q, im, cols].astype(F32)
                u_re, u_im = ue[q, re, at : at + size].astype(F32), ue[q, im, at : at + size].astype(F32)
                if which:
                    prod[q, re, cols] = (w_re * u_re + w_im * u_im).astype(BF16)
                    prod[q, im, cols] = (w_re * u_im - w_im * u_re).astype(BF16)
                else:
                    prod[q, re, cols] = (w_re * u_re - w_im * u_im).astype(BF16)
                    prod[q, im, cols] = (w_re * u_im + w_im * u_re).astype(BF16)
            return 0

        lax.fori_loop(0, MODES, body, 0)
        summed = (dot(prod[0], collapse[0]) + dot(prod[1], collapse[1])).astype(BF16)
        lined = jnp.concatenate([summed[b * ROWS : (b + 1) * ROWS] for b in range(HALF)], axis=1)
        return dot(lined, tab["place"][...]).astype(BF16)

    own_block = pl.ds(pl.multiple_of(px * BLOCK, BLOCK), BLOCK)

    def inverse_send(t, mixed):
        spatial = dot(tab["myt"][...], mixed).astype(BF16)
        mine = pl.ds(pl.multiple_of(px * BLOCK + py * PIECE, PIECE), PIECE)
        for g in range(GROUPS):
            vbuf[t, g] = spatial[:, g * LANES : (g + 1) * LANES]
            for k in range(1, PY):
                dest = lax.rem(py + k, PY)
                rows = pl.ds(pl.multiple_of(dest * PIECE, PIECE), PIECE)
                a2_c[2 * t + 1, g, k] = send(
                    vbuf.at[t, g, rows], ag.at[t, g, mine],
                    a2_s.at[2 * t + 1, g, k - 1], a2_r.at[2 * t + 1, g, k - 1], at_py(k),
                )
            here = pl.ds(pl.multiple_of(py * PIECE, PIECE), PIECE)
            ag[t, g, mine, :] = vbuf[t, g, here, :]

    def gather_send(t, g):
        for k in range(1, PY):
            a2_c[2 * t + 1, g, k].wait_recv()
        for j in (2, 1, 3):
            ag_c[t, g, j] = send(
                ag.at[t, g, own_block], ag.at[t, g, own_block], ag_s.at[t, g, j - 1], ag_r.at[t, g, j - 1], at_px(j)
            )

    def cross_back(t, g):
        for j in range(1, PX):
            ag_c[t, g, j].wait_recv()

        wide_ag[...] = ag[t, g].astype(F32)
        for y in range(YL):
            xbuf[:, y * LANES : (y + 1) * LANES] = wide_ag[pl.ds(y, 2 * KX, stride=YL), :].astype(BF16)
        made = dot(tab["m1t"][...], xbuf[...])
        for y in range(YL):
            back[y * 2 * XL : (y + 1) * 2 * XL, :] = made[:, y * LANES : (y + 1) * LANES]
        for x in range(XL):
            for s in range(2):
                tbuf[x * YL : (x + 1) * YL, s * LANES : (s + 1) * LANES] = back[
                    pl.ds(s * XL + x, YL, stride=2 * XL), :
                ].astype(BF16)

    def field_values(table):
        made = dot(tbuf[...], table[...])
        for c in range(GC):
            zval[c] = made[:, c * NZ : (c + 1) * NZ]

    def bypass_part(matrix, source, first, last):
        def body(b, _):
            parts = []
            for e in range(2):
                rows = pl.ds(pl.multiple_of(b * 32 + e * 16, 16), 16)
                parts.append(source[:, rows, :].reshape(CH * YL, NZ))
            value = dot(matrix[...], jnp.concatenate(parts, axis=1))
            for e in range(2):
                rows = pl.ds(pl.multiple_of(b * 32 + e * 16, 16), 16)
                pb[:, rows, :] = value[:, e * NZ : (e + 1) * NZ].reshape(CH, YL, NZ)
            return 0

        lax.fori_loop(first, last, body, 0)

    def share(name, n, data):
        for j in range(1, 4):
            dp_c[name, j] = send(data.at[0], data.at[j], dp_s.at[n, j], dp_r.at[n, j], at_y(j))
        dp_c[name, 4] = send(data.at[0], data.at[4], dp_s.at[n, 4], dp_r.at[n, 4], far)

    def share_far(name, n, data):
        dp_c[name, 4].wait_recv()
        for j in range(1, 4):
            dp_c[name, 4 + j] = send(data.at[4], data.at[4 + j], dp_s.at[n, 4 + j], dp_r.at[n, 4 + j], at_y(j))

    need("f0", "dz", "m1")
    load("f1", fields_h.at[pl.ds(GC, GC)], fields.at[pl.ds(GC, GC)], 3)
    load("f2", fields_h.at[pl.ds(2 * GC, GC)], fields.at[pl.ds(2 * GC, GC)], 4)
    load("w", w_h, w4, 5)
    load("m1t", tab_h["m1t"].at[px], tab["m1t"], 6)
    for g in range(GROUPS):
        need("f%d" % g)
        if g == GROUPS - 1:
            load_later()

        depth(fields, g, tab["dz"])
        if g == 0:
            pl.semaphore_wait(barrier, len(partners))
        cross_and_send(0, g)

    need("rep", "rept")
    mask = lax.rem(lax.broadcasted_iota(jnp.int32, (CH * YL, CH * YL), 0), YL) == lax.rem(
        lax.broadcasted_iota(jnp.int32, (CH * YL, CH * YL), 1), YL
    )
    left = dot(tab["rep"][...], byp[...]).astype(BF16)
    full = dot(left, tab["rept"][...])
    bypk[...] = jnp.where(mask, full, 0.0).astype(BF16)
    bypkt[...] = jnp.where(mask, full, 0.0).T.astype(BF16)

    need("w")

    def weight_rows(b, _):
        for q in range(2):
            for part in range(2):
                w[q, pl.ds(pl.multiple_of(b * ROWS + part * KY, KY), KY), :] = w4[:, 2 * b + q, part, :]
        return 0

    lax.fori_loop(0, HALF // 2, weight_rows, 0)
    reduce_and_send(0, 0)
    lax.fori_loop(HALF // 2, HALF, weight_rows, 0)
    reduce_and_send(0, 1)
    reduce_and_send(0, 2)

    need("my", "sel", "expand", "sum_o", "place", "myt")
    u_hat = spectrum(0)
    dpu[0] = u_hat
    share("u", 0, dpu)
    spread(u_hat, 0)
    inverse_send(0, mix(0, tab["sum_o"]))
    bypass_part(bypk, fields, 0, 9)
    need("m1t", "dht", "dh", "cot")
    for g in range(GROUPS):
        gather_send(0, g)
    share_far("u", 0, dpu)
    bypass_part(bypk, fields, 9, CELLS // 32)

    for g in range(GROUPS):
        cross_back(0, g)
        field_values(tab["dht"])

        def body(r, _):
            rows = pl.ds(pl.multiple_of(r * CHUNK, CHUNK), CHUNK)
            for c in range(GC):
                pre = zval[c, rows, :] + pb[g * GC + c, rows, :]
                slope = gelu_slope(pre)
                gp[g * GC + c, rows, :] = (cot[g * GC + c, rows, :].astype(F32) * slope).astype(BF16)
            return 0

        lax.fori_loop(0, CELLS // CHUNK, body, 0)
        depth(gp, g, tab["dh"])
        cross_and_send(1, g)
        if g:
            reduce_and_send(1, g - 1)
    bypass_part(bypkt, gp, 0, CELLS // 32)
    reduce_and_send(1, GROUPS - 1)

    need("sum_i", "dzt")
    g_hat = spectrum(1)
    dpg[0] = g_hat
    share("g", 1, dpg)
    spread(g_hat, 1)
    inverse_send(1, mix(1, tab["sum_i"]))

    def choose(h):
        for j in range(NEAR * h, NEAR * (h + 1)):
            if j:
                if h == 0 or j > NEAR:
                    dp_c["u", j].wait_recv()
                    dp_c["g", j].wait_recv()
        part = slice(NEAR * h, NEAR * (h + 1))
        both = jnp.concatenate(
            [dpu[part].reshape(NEAR * ROWS, CH * MODES), dpg[part].reshape(NEAR * ROWS, CH * MODES)], axis=1
        )
        chosen = dot(both, tab["sel"][...]).astype(BF16)
        for b in range(HALF):
            gs[b] = chosen[:, b * 128 : (b + 1) * 128]

    def gw_part(h, first, last):
        def gw_body(b, _):
            for q in range(2):
                wide[...] = dot(gs[b], tab["expand"][q])
                for v in range(WIDE // 128):
                    cols = slice(v * 128, min((v + 1) * 128, IO))
                    size = cols.stop - cols.start
                    at = WIDE + (v % 3) * 128
                    real = acc[2 * b + q, 0, :, cols] if h else None
                    imag = acc[2 * b + q, 1, :, cols] if h else None
                    for d in range(NEAR):
                        re = slice(d * ROWS, d * ROWS + KY)
                        im = slice(d * ROWS + KY, (d + 1) * ROWS)
                        u_re, u_im = wide[re, cols], wide[im, cols]
                        g_re, g_im = wide[re, at : at + size], wide[im, at : at + size]
                        more_real = g_re * u_re + g_im * u_im
                        more_imag = g_im * u_re - g_re * u_im
                        real = more_real if real is None else real + more_real
                        imag = more_imag if imag is None else imag + more_imag
                    if h:
                        gw[:, 2 * b + q, 0, cols] = real
                        gw[:, 2 * b + q, 1, cols] = imag
                    else:
                        acc[2 * b + q, 0, :, cols] = real
                        acc[2 * b + q, 1, :, cols] = imag
            return 0

        lax.fori_loop(first, last, gw_body, 0)

    choose(0)
    gw_part(0, 0, 3)
    gather_send(1, 0)
    share_far("g", 1, dpg)
    gather_send(1, 1)
    gather_send(1, 2)
    gw_part(0, 3, HALF)

    stores = []

    def finish(g):
        cross_back(1, g)
        field_values(tab["dzt"])

        def body(r, _):
            rows = pl.ds(pl.multiple_of(r * CHUNK, CHUNK), CHUNK)
            for c in range(GC):
                out[g * GC + c, rows, :] = (zval[c, rows, :] + pb[g * GC + c, rows, :]).astype(BF16)
            return 0

        lax.fori_loop(0, CELLS // CHUNK, body, 0)
        part = pl.ds(g * GC, GC)
        copy = pltpu.make_async_copy(out.at[part], gf_h.at[part], store_sem.at[g])
        copy.start()
        stores.append(copy)

    finish(0)

    choose(1)
    gw_part(1, 0, HALF)
    stores.append(pltpu.make_async_copy(gw, gw_h, store_sem.at[GROUPS]))
    stores[-1].start()

    finish(1)
    finish(2)

    for copy in stores:
        copy.wait()
    for copy in sends:
        copy.wait_send()


def shards(fields, cotangent, spectral_weight, bypass):
    tab = tables()
    arrays = [jnp.asarray(tab[name]) for name in NAMES]
    any_spec = pl.BlockSpec(memory_space=pl.ANY)
    vmem = pltpu.VMEM
    shapes = [a.shape[1:] if name in ("m1", "m1t") else a.shape for name, a in zip(NAMES, arrays)]
    scratch = [vmem(shape, BF16) for shape in shapes] + [
        vmem((CH, CELLS, NZ), BF16),
        vmem((CH, CELLS, NZ), BF16),
        vmem((CH, CELLS, NZ), BF16),
        vmem((KY, MODES, 2, IO), BF16),
        vmem((2, HALF * ROWS, IO), BF16),
        vmem((CH, CELLS, NZ), F32),
        vmem((CH, CELLS, NZ), BF16),
        vmem((CH * YL, CH * YL), BF16),
        vmem((CH * YL, CH * YL), BF16),
        vmem((2 * XL, YLANES), BF16),
        vmem((CELLS, 2 * LANES), BF16),
        vmem((GC, CELLS, NZ), F32),
        vmem((2, CELLS, LANES), F32),
        vmem((YL * XROWS, LANES), F32),
        vmem((YL * 2 * XL, LANES), F32),
        vmem((2 * KX * YL, LANES), F32),
        vmem((2, GROUPS, PX, XROWS, YLANES), BF16),
        vmem((2, GROUPS, PX - 1, XROWS, YLANES), BF16),
        vmem((2, GROUPS, BLOCK, LANES), BF16),
        vmem((2, GROUPS, BLOCK, LANES), BF16),
        vmem((2, GROUPS, BLOCK, LANES), BF16),
        vmem((2, GROUPS, PX * BLOCK, LANES), BF16),
        vmem((DP, ROWS, CH * MODES), BF16),
        vmem((DP, ROWS, CH * MODES), BF16),
        vmem((2, HALF * ROWS, WIDE), BF16),
        vmem((2, HALF * ROWS, IO), BF16),
        vmem((HALF * ROWS, 128), BF16),
        vmem((HALF, NEAR * ROWS, 128), BF16),
        vmem((NEAR * ROWS, WIDE + PATTERN), F32),
        vmem((MODES, 2, KY, WIDE), F32),
        vmem((KY, MODES, 2, IO), F32),
        pltpu.SemaphoreType.DMA((len(NAMES) + 5,)),
        pltpu.SemaphoreType.DMA((GROUPS + 1,)),
        pltpu.SemaphoreType.DMA((2, GROUPS, PX - 1)),
        pltpu.SemaphoreType.DMA((2, GROUPS, PX - 1)),
        pltpu.SemaphoreType.DMA((4, GROUPS, PY - 1)),
        pltpu.SemaphoreType.DMA((4, GROUPS, PY - 1)),
        pltpu.SemaphoreType.DMA((2, GROUPS, PX - 1)),
        pltpu.SemaphoreType.DMA((2, GROUPS, PX - 1)),
        pltpu.SemaphoreType.DMA((2, DP)),
        pltpu.SemaphoreType.DMA((2, DP)),
    ]
    gw, gf = pl.pallas_call(
        kernel,
        out_shape=(
            jax.ShapeDtypeStruct((KY, MODES, 2, IO), F32),
            jax.ShapeDtypeStruct((CH, CELLS, NZ), BF16),
        ),
        in_specs=[any_spec] * 3 + [pl.BlockSpec(memory_space=pltpu.VMEM)] + [any_spec] * len(arrays),
        out_specs=(any_spec, any_spec),
        scratch_shapes=scratch,
        compiler_params=pltpu.CompilerParams(
            collective_id=0, has_side_effects=True, vmem_limit_bytes=60 * 1024 * 1024
        ),
        cost_estimate=pl.CostEstimate(flops=20_000_000_000, bytes_accessed=30_000_000, transcendentals=3_000_000),
    )(
        fields.reshape(CH, CELLS, NZ), cotangent.reshape(CH, CELLS, NZ), spectral_weight, bypass, *arrays
    )
    return gw, gf.reshape(1, CH, XL, YL, NZ)


def solution(mesh):
    in_specs = (
        P("dp", None, "px", "py", None),
        P("dp", None, "px", "py", None),
        P(("px", "py"), None, None, None),
        P(),
    )
    out_specs = (P(("px", "py"), None, None, None), P("dp", None, "px", "py", None))
    return jax.shard_map(shards, mesh=mesh, in_specs=in_specs, out_specs=out_specs, check_vma=False)
```

time: 109 us -> 89.5 us (0.82); the launches traced: 107 us -> 89.3 us
  Pallas kernels: 96.8 us -> 82.7 us
  local copies, waits for them, and re-layouts: 9.86 us -> 5.95 us
    pallas_call x1, Pallas kernels: 96.8 us -> 82.7 us  [shards(): pl.pallas_call(kernel, out_shape=(jax.ShapeDtypeStruct((KY, MODES, 2, IO)...]
    reshape x1 -> x0, local copies, waits for them, and re-layouts: 5.4 us -> none  [shards(): grad_weight = gw.reshape(MODES, 2, KY, IO).transpose(2, 0, 1, 3)]
    unnamed x3 -> x4, local copies, waits for them, and re-layouts: 1.67 us -> 5.95 us
    transpose x1 -> x0, local copies, waits for them, and re-layouts: 2.78 us -> none  [shards(): w = spectral_weight.transpose(1, 2, 0, 3).reshape(MODES * ROWS, IO)]
where the time goes in v2:
time: 89.5 us; the launch traced here: 89.3 us
  Pallas kernels  82.7 us (92%)
  local copies, waits for them, and re-layouts  5.95 us (7%)
    pallas_call x1, Pallas kernels, shards(): pl.pallas_call(kernel, out_shape=(jax.ShapeDtypeStruct((KY, MODES, 2, IO)...  82.7 us
    unnamed x4, local copies, waits for them, and re-layouts  5.95 us

profile of v2, /device:TPU:2, one launch (start us, length us, event | category | flops | bytes accessed | tf_op | source)
XLA Modules:
  0.0 89.3 jit_solution(3931494872081141580)
XLA Ops:
  0.6 82.7 %shard_map.194 = (f32[32,16,2,576]{3,2,1,0:T(2,128)}, bf16[24,512,128]{2,1,0:T(8,128)(2,1)}) custom-call(bf16[24,512,128]{2,1,0:T(8,128)(2,1)} %bitcast.4, bf16[24,512,128]{2,1,0:T(8,128)(2,1)} %bitcast.5, bf16[32,16,2,576]{3,2,1,0:T(2,128)(2,1)} %refs_2_.1, bf16[24,24]{1,0:T(8,128)(2,1)} %refs_3_.1, bf16[1024,256]{1,0:T(8,128)(2,1)} %constant.30.clone.refs_4_, ...), custom_call_target="tpu_custom_call" | custom-call | flops 20000000000 | bytes 30000000 | tf_op jit(solution)/shard_map/pallas_call | solution.py:582
  83.4 0.0 copy-start
  83.4 4.3 %copy.23 = f32[32,16,2,576]{3,2,1,0:T(2,128)} copy(f32[32,16,2,576]{3,2,1,0:T(2,128)} %get-tuple-element.8) | data formatting | bytes 4718592
  87.7 0.0 copy-done
  87.7 1.7 %copy.24 = bf16[1,24,32,16,128]{4,3,2,1,0:T(8,128)(2,1)} copy(bf16[1,24,32,16,128]{4,3,2,1,0:T(8,128)(2,1)S(1)} %bitcast.3) | data formatting | bytes 6291456
Async XLA Ops:
  83.4 4.3 %copy-start = (bf16[24,512,128]{2,1,0:T(8,128)(2,1)S(1)}, bf16[24,512,128]{2,1,0:T(8,128)(2,1)}, u32[]{:S(2)}) copy-start(bf16[24,512,128]{2,1,0:T(8,128)(2,1)} %get-tuple-element.5) | copy-start | bytes 9437188

commit v3 on v2

--- a/solution.py
+++ b/solution.py
@@ -145,15 +145,42 @@
     return normal_cdf + values * density
 
 
+def group_values(block, m1t, table, wide_ag, xbuf, back, tbuf, zval):
+    wide_ag[...] = block.astype(F32)
+    for y in range(YL):
+        xbuf[:, y * LANES : (y + 1) * LANES] = wide_ag[pl.ds(y, 2 * KX, stride=YL), :].astype(BF16)
+    made = dot(m1t[...], xbuf[...])
+    for y in range(YL):
+        back[y * 2 * XL : (y + 1) * 2 * XL, :] = made[:, y * LANES : (y + 1) * LANES]
+    for x in range(XL):
+        for s in range(2):
+            tbuf[x * YL : (x + 1) * YL, s * LANES : (s + 1) * LANES] = back[
+                pl.ds(s * XL + x, YL, stride=2 * XL), :
+            ].astype(BF16)
+    made = dot(tbuf[...], table[...])
+    for c in range(GC):
+        zval[c] = made[:, c * NZ : (c + 1) * NZ]
+
+
+def add_bypass(zval, bypass_values, out, first, last):
+    def body(r, _):
+        rows = pl.ds(pl.multiple_of(r * CHUNK, CHUNK), CHUNK)
+        for c in range(GC):
+            out[c, rows, :] = (zval[c, rows, :] + bypass_values[c, rows, :].astype(F32)).astype(BF16)
+        return 0
+
+    lax.fori_loop(first, last, body, 0)
+
+
 def kernel(*refs):
     fields_h, cot_h, w_h, byp = refs[:4]
     tab_h = dict(zip(NAMES, refs[4 : 4 + len(NAMES)]))
     refs = refs[4 + len(NAMES) :]
-    gw_h, gf_h = refs[:2]
-    refs = refs[2:]
+    gw_h, gf_h, ag_h, pb_h = refs[:4]
+    refs = refs[4:]
     tab = dict(zip(NAMES, refs[: len(NAMES)]))
     (
-        fields, cot, gp, w4, w, pb, out, bypk, bypkt, xbuf, tbuf, zval, lines, turn, back, wide_ag, ybuf, rs, sbuf, rbuf, vbuf, ag, dpu, dpg,
+        fields, cot, gp, w4, w, pb, pb16, out, bypk, bypkt, xbuf, tbuf, zval, lines, turn, back, wide_ag, ybuf, rs, sbuf, rbuf, vbuf, ag, dpu, dpg,
         ue, prod, us, gs, wide, acc, gw,
         load_sem, store_sem, rs_s, rs_r, a2_s, a2_r, ag_s, ag_r, dp_s, dp_r,
     ) = refs[len(NAMES) :]
@@ -326,24 +353,11 @@
         for j in range(1, PX):
             ag_c[t, g, j].wait_recv()
 
-        wide_ag[...] = ag[t, g].astype(F32)
-        for y in range(YL):
-            xbuf[:, y * LANES : (y + 1) * LANES] = wide_ag[pl.ds(y, 2 * KX, stride=YL), :].astype(BF16)
-        made = dot(tab["m1t"][...], xbuf[...])
-        for y in range(YL):
-            back[y * 2 * XL : (y + 1) * 2 * XL, :] = made[:, y * LANES : (y + 1) * LANES]
-        for x in range(XL):
-            for s in range(2):
-                tbuf[x * YL : (x + 1) * YL, s * LANES : (s + 1) * LANES] = back[
-                    pl.ds(s * XL + x, YL, stride=2 * XL), :
-                ].astype(BF16)
-
-    def field_values(table):
-        made = dot(tbuf[...], table[...])
-        for c in range(GC):
-            zval[c] = made[:, c * NZ : (c + 1) * NZ]
-
-    def bypass_part(matrix, source, first, last):
+        group_values(
+            ag[t, g], tab["m1t"], tab["dht" if t == 0 else "dzt"], wide_ag, xbuf, back, tbuf, zval
+        )
+
+    def bypass_part(matrix, source, target, first, last):
         def body(b, _):
             parts = []
             for e in range(2):
@@ -352,7 +366,7 @@
             value = dot(matrix[...], jnp.concatenate(parts, axis=1))
             for e in range(2):
                 rows = pl.ds(pl.multiple_of(b * 32 + e * 16, 16), 16)
-                pb[:, rows, :] = value[:, e * NZ : (e + 1) * NZ].reshape(CH, YL, NZ)
+                target[:, rows, :] = value[:, e * NZ : (e + 1) * NZ].reshape(CH, YL, NZ).astype(target.dtype)
             return 0
 
         lax.fori_loop(first, last, body, 0)
@@ -411,16 +425,15 @@
     share("u", 0, dpu)
     spread(u_hat, 0)
     inverse_send(0, mix(0, tab["sum_o"]))
-    bypass_part(bypk, fields, 0, 9)
+    bypass_part(bypk, fields, pb, 0, 9)
     need("m1t", "dht", "dh", "cot")
     for g in range(GROUPS):
         gather_send(0, g)
     share_far("u", 0, dpu)
-    bypass_part(bypk, fields, 9, CELLS // 32)
+    bypass_part(bypk, fields, pb, 9, CELLS // 32)
 
     for g in range(GROUPS):
         cross_back(0, g)
-        field_values(tab["dht"])
 
         def body(r, _):
             rows = pl.ds(pl.multiple_of(r * CHUNK, CHUNK), CHUNK)
@@ -435,7 +448,9 @@
         cross_and_send(1, g)
         if g:
             reduce_and_send(1, g - 1)
-    bypass_part(bypkt, gp, 0, CELLS // 32)
+    bypass_part(bypkt, gp, pb16, 0, CELLS // 32)
+    stores = [pltpu.make_async_copy(pb16.at[pl.ds(GC, 2 * GC)], pb_h, store_sem.at[0])]
+    stores[0].start()
     reduce_and_send(1, GROUPS - 1)
 
     need("sum_i", "dzt")
@@ -492,42 +507,74 @@
     gw_part(0, 0, 3)
     gather_send(1, 0)
     share_far("g", 1, dpg)
+    gw_part(0, 3, 5)
     gather_send(1, 1)
     gather_send(1, 2)
-    gw_part(0, 3, HALF)
-
-    stores = []
-
-    def finish(g):
-        cross_back(1, g)
-        field_values(tab["dzt"])
-
-        def body(r, _):
-            rows = pl.ds(pl.multiple_of(r * CHUNK, CHUNK), CHUNK)
-            for c in range(GC):
-                out[g * GC + c, rows, :] = (zval[c, rows, :] + pb[g * GC + c, rows, :]).astype(BF16)
-            return 0
-
-        lax.fori_loop(0, CELLS // CHUNK, body, 0)
-        part = pl.ds(g * GC, GC)
-        copy = pltpu.make_async_copy(out.at[part], gf_h.at[part], store_sem.at[g])
-        copy.start()
-        stores.append(copy)
-
-    finish(0)
+    gw_part(0, 5, HALF)
+
+    cross_back(1, 0)
+    for h in range(2):
+        add_bypass(zval, pb16, out, h * CELLS // CHUNK // 2, (h + 1) * CELLS // CHUNK // 2)
+        part = (slice(None), pl.ds(h * CELLS // 2, CELLS // 2))
+        stores.append(pltpu.make_async_copy(out.at[part], gf_h.at[part], store_sem.at[1 + h]))
+        stores[-1].start()
 
     choose(1)
     gw_part(1, 0, HALF)
-    stores.append(pltpu.make_async_copy(gw, gw_h, store_sem.at[GROUPS]))
+    stores.append(pltpu.make_async_copy(gw, gw_h, store_sem.at[3]))
     stores[-1].start()
-
-    finish(1)
-    finish(2)
+    for g in range(1, GROUPS):
+        for j in range(1, PX):
+            ag_c[1, g, j].wait_recv()
+        stores.append(pltpu.make_async_copy(ag.at[1, g], ag_h.at[g - 1], store_sem.at[3 + g]))
+        stores[-1].start()
 
     for copy in stores:
         copy.wait()
     for copy in sends:
         copy.wait_send()
+
+
+def last_groups(gw_in, gf_in, ag_in, pb_in, m1t_h, dzt_h, gw_out, gf_out,
+                gw, gf, ag, pb, m1t, dzt, wide_ag, xbuf, back, tbuf, zval, sem, out_sem):
+    px = lax.axis_index("px")
+    pairs = [
+        (ag_in.at[0], ag.at[0]), (m1t_h.at[px], m1t), (dzt_h, dzt),
+        (pb_in.at[pl.ds(0, GC)], pb.at[pl.ds(0, GC)]), (gw_in, gw), (ag_in.at[1], ag.at[1]),
+        (pb_in.at[pl.ds(GC, GC)], pb.at[pl.ds(GC, GC)]), (gf_in, gf.at[pl.ds(0, GC)]),
+    ]
+    reads = [pltpu.make_async_copy(src, dst, sem.at[n]) for n, (src, dst) in enumerate(pairs)]
+    for read in reads:
+        read.start()
+    writes = []
+
+    def write(src, dst):
+        writes.append(pltpu.make_async_copy(src, dst, out_sem.at[len(writes)]))
+        writes[-1].start()
+
+    for n in range(3):
+        reads[n].wait()
+    for g in range(1, GROUPS):
+        if g == 2:
+            reads[5].wait()
+        group_values(ag[g - 1], m1t, dzt, wide_ag, xbuf, back, tbuf, zval)
+        reads[3 if g == 1 else 6].wait()
+        part = pl.ds(g * GC, GC)
+        if g == 1:
+            reads[4].wait()
+            write(gw, gw_out)
+        for h in range(2):
+            add_bypass(
+                zval, pb.at[pl.ds((g - 1) * GC, GC)], gf.at[part],
+                h * CELLS // CHUNK // 2, (h + 1) * CELLS // CHUNK // 2,
+            )
+            rows = pl.ds(h * CELLS // 2, CELLS // 2)
+            write(gf.at[part, rows], gf_out.at[part, rows])
+        if g == 1:
+            reads[7].wait()
+            write(gf.at[pl.ds(0, GC)], gf_out.at[pl.ds(0, GC)])
+    for copy in writes:
+        copy.wait()
 
 
 def shards(fields, cotangent, spectral_weight, bypass):
@@ -544,6 +591,7 @@
         vmem((2, HALF * ROWS, IO), BF16),
         vmem((CH, CELLS, NZ), F32),
         vmem((CH, CELLS, NZ), BF16),
+        vmem((GC, CELLS, NZ), BF16),
         vmem((CH * YL, CH * YL), BF16),
         vmem((CH * YL, CH * YL), BF16),
         vmem((2 * XL, YLANES), BF16),
@@ -569,7 +617,7 @@
         vmem((MODES, 2, KY, WIDE), F32),
         vmem((KY, MODES, 2, IO), F32),
         pltpu.SemaphoreType.DMA((len(NAMES) + 5,)),
-        pltpu.SemaphoreType.DMA((GROUPS + 1,)),
+        pltpu.SemaphoreType.DMA((6,)),
         pltpu.SemaphoreType.DMA((2, GROUPS, PX - 1)),
         pltpu.SemaphoreType.DMA((2, GROUPS, PX - 1)),
         pltpu.SemaphoreType.DMA((4, GROUPS, PY - 1)),
@@ -579,14 +627,16 @@
         pltpu.SemaphoreType.DMA((2, DP)),
         pltpu.SemaphoreType.DMA((2, DP)),
     ]
-    gw, gf = pl.pallas_call(
+    gw, gf, ag, pb = pl.pallas_call(
         kernel,
         out_shape=(
             jax.ShapeDtypeStruct((KY, MODES, 2, IO), F32),
-            jax.ShapeDtypeStruct((CH, CELLS, NZ), BF16),
+            jax.ShapeDtypeStruct((GC, CELLS, NZ), BF16),
+            jax.ShapeDtypeStruct((2, PX * BLOCK, LANES), BF16),
+            jax.ShapeDtypeStruct((2 * GC, CELLS, NZ), BF16),
         ),
         in_specs=[any_spec] * 3 + [pl.BlockSpec(memory_space=pltpu.VMEM)] + [any_spec] * len(arrays),
-        out_specs=(any_spec, any_spec),
+        out_specs=(any_spec,) * 4,
         scratch_shapes=scratch,
         compiler_params=pltpu.CompilerParams(
             collective_id=0, has_side_effects=True, vmem_limit_bytes=60 * 1024 * 1024
@@ -595,6 +645,32 @@
     )(
         fields.reshape(CH, CELLS, NZ), cotangent.reshape(CH, CELLS, NZ), spectral_weight, bypass, *arrays
     )
+    gw, gf = pl.pallas_call(
+        last_groups,
+        out_shape=(
+            jax.ShapeDtypeStruct((KY, MODES, 2, IO), F32),
+            jax.ShapeDtypeStruct((CH, CELLS, NZ), BF16),
+        ),
+        in_specs=[any_spec] * 6,
+        out_specs=(any_spec, any_spec),
+        scratch_shapes=[
+            vmem((KY, MODES, 2, IO), F32),
+            vmem((CH, CELLS, NZ), BF16),
+            vmem((2, PX * BLOCK, LANES), BF16),
+            vmem((2 * GC, CELLS, NZ), BF16),
+            vmem((2 * XL, 2 * KX), BF16),
+            vmem((2 * LANES, GC * NZ), BF16),
+            vmem((2 * KX * YL, LANES), F32),
+            vmem((2 * XL, YLANES), BF16),
+            vmem((YL * 2 * XL, LANES), F32),
+            vmem((CELLS, 2 * LANES), BF16),
+            vmem((GC, CELLS, NZ), F32),
+            pltpu.SemaphoreType.DMA((8,)),
+            pltpu.SemaphoreType.DMA((6,)),
+        ],
+        compiler_params=pltpu.CompilerParams(vmem_limit_bytes=56 * 1024 * 1024),
+        cost_estimate=pl.CostEstimate(flops=1_000_000_000, bytes_accessed=12_000_000, transcendentals=0),
+    )(gw, gf, ag, pb, jnp.asarray(tab["m1t"]), jnp.asarray(tab["dzt"]))
     return gw, gf.reshape(1, CH, XL, YL, NZ)
 
 

time: 89.5 us -> 88.3 us (0.987); the launches traced: 89.3 us -> 87 us
  local copies, waits for them, and re-layouts: 5.95 us -> 0 us
  Pallas kernels: 82.7 us -> 86.2 us
    unnamed x4 -> x0, local copies, waits for them, and re-layouts: 5.95 us -> none
    pallas_call x0 -> x1, Pallas kernels: none -> 5.15 us  [shards(): pl.pallas_call(last_groups, out_shape=(jax.ShapeDtypeStruct((KY, MODES, 2...]
    pallas_call x1, Pallas kernels: 82.7 us -> 81 us  [shards(): pl.pallas_call(kernel, out_shape=(jax.ShapeDtypeStruct((KY, MODES, 2, IO)...]
where the time goes in v3:
time: 88.3 us; the launch traced here: 87 us
  Pallas kernels  86.2 us (98%)
    pallas_call x1, Pallas kernels, shards(): pl.pallas_call(kernel, out_shape=(jax.ShapeDtypeStruct((KY, MODES, 2, IO)...  81 us
    pallas_call x1, Pallas kernels, shards(): pl.pallas_call(last_groups, out_shape=(jax.ShapeDtypeStruct((KY, MODES, 2...  5.15 us

profile of v3, /device:TPU:2, one launch (start us, length us, event | category | flops | bytes accessed | tf_op | source)
XLA Modules:
  0.0 87.0 jit_solution(12890102678330707133)
XLA Ops:
  0.6 81.0 %shard_map.194 = (f32[32,16,2,576]{3,2,1,0:T(2,128)}, bf16[8,512,128]{2,1,0:T(8,128)(2,1)}, bf16[2,1024,128]{2,1,0:T(8,128)(2,1)}, bf16[16,512,128]{2,1,0:T(8,128)(2,1)}) custom-call(bf16[24,512,128]{2,1,0:T(8,128)(2,1)} %bitcast.3, bf16[24,512,128]{2,1,0:T(8,128)(2,1)} %bitcast.4, bf16[32,16,2,576]{3,2,1,0:T(2,128)(2,1)} %refs_2_.1, ...), custom_call_target="tpu_custom_call" | custom-call | flops 20000000000 | bytes 30000000 | tf_op jit(solution)/shard_map/pallas_call | solution.py:630
  81.7 5.2 %shard_map.195 = (f32[32,16,2,576]{3,2,1,0:T(2,128)}, bf16[24,512,128]{2,1,0:T(8,128)(2,1)}) custom-call(f32[32,16,2,576]{3,2,1,0:T(2,128)} %get-tuple-element.8.gw_in, bf16[8,512,128]{2,1,0:T(8,128)(2,1)} %get-tuple-element.9.gf_in, bf16[2,1024,128]{2,1,0:T(8,128)(2,1)} %get-tuple-element.10.ag_in, bf16[16,512,128]{2,1,0:T(8,128)(2,1)} %get-tuple-element.11.pb_in, ...), custom_call_target="tpu_custom_call" | custom-call | flops 1000000000 | bytes 12000000 | tf_op jit(solution)/shard_map/pallas_call | solution.py:648

commit v4 on v3

--- a/solution.py
+++ b/solution.py
@@ -544,7 +544,7 @@
         (pb_in.at[pl.ds(GC, GC)], pb.at[pl.ds(GC, GC)]), (gf_in, gf.at[pl.ds(0, GC)]),
     ]
     reads = [pltpu.make_async_copy(src, dst, sem.at[n]) for n, (src, dst) in enumerate(pairs)]
-    for read in reads:
+    for read in reads[:4]:
         read.start()
     writes = []
 
@@ -554,6 +554,8 @@
 
     for n in range(3):
         reads[n].wait()
+    for read in reads[4:]:
+        read.start()
     for g in range(1, GROUPS):
         if g == 2:
             reads[5].wait()

time: 88.3 us -> 89 us (level)
  no operation moved by 1% of the time
where the time goes in v4:
time: 89 us; the launch traced here: 87.7 us
  Pallas kernels  86.8 us (98%)
    pallas_call x1, Pallas kernels, shards(): pl.pallas_call(kernel, out_shape=(jax.ShapeDtypeStruct((KY, MODES, 2, IO)...  81 us
    pallas_call x1, Pallas kernels, shards(): pl.pallas_call(last_groups, out_shape=(jax.ShapeDtypeStruct((KY, MODES, 2...  5.8 us

profile of v4, /device:TPU:2, one launch (start us, length us, event | category | flops | bytes accessed | tf_op | source)
XLA Modules:
  0.0 87.7 jit_solution(7714365903547649842)
XLA Ops:
  0.6 81.0 %shard_map.194 = (f32[32,16,2,576]{3,2,1,0:T(2,128)}, bf16[8,512,128]{2,1,0:T(8,128)(2,1)}, bf16[2,1024,128]{2,1,0:T(8,128)(2,1)}, bf16[16,512,128]{2,1,0:T(8,128)(2,1)}) custom-call(bf16[24,512,128]{2,1,0:T(8,128)(2,1)} %bitcast.3, bf16[24,512,128]{2,1,0:T(8,128)(2,1)} %bitcast.4, bf16[32,16,2,576]{3,2,1,0:T(2,128)(2,1)} %refs_2_.1, ...), custom_call_target="tpu_custom_call" | custom-call | flops 20000000000 | bytes 30000000 | tf_op jit(solution)/shard_map/pallas_call | solution.py:632
  81.7 5.8 %shard_map.195 = (f32[32,16,2,576]{3,2,1,0:T(2,128)}, bf16[24,512,128]{2,1,0:T(8,128)(2,1)}) custom-call(f32[32,16,2,576]{3,2,1,0:T(2,128)} %get-tuple-element.8.gw_in, bf16[8,512,128]{2,1,0:T(8,128)(2,1)} %get-tuple-element.9.gf_in, bf16[2,1024,128]{2,1,0:T(8,128)(2,1)} %get-tuple-element.10.ag_in, bf16[16,512,128]{2,1,0:T(8,128)(2,1)} %get-tuple-element.11.pb_in, ...), custom_call_target="tpu_custom_call" | custom-call | flops 1000000000 | bytes 12000000 | tf_op jit(solution)/shard_map/pallas_call | solution.py:650
